TPU v7x, 32 devices: a whole 2x2x4 slice. The times are simulated.
32 devices in a mesh: groups: 2 (over y), ep: 4 (over z), half: 2 (over x), tp: 2 (over core).
Axes of the slice: x: 2, y: 2, z: 4, core: 2. Of those that a mesh axis runs over, the one named last changes fastest.
Arguments:
- queries: bfloat16 [512, 2048], P(('groups', 'ep', 'half'), 'tp'), parts along dimension 0, may hold values from -6 to 6
- new_keys: bfloat16 [512, 256], P(('groups', 'ep', 'half'), 'tp'), parts along dimension 0, may hold values from -4 to 4
- new_values: bfloat16 [512, 256], P(('groups', 'ep', 'half'), 'tp'), parts along dimension 0, may hold values from -4 to 4
- cache_keys: bfloat16 [512, 2, 64, 128], P(('groups', 'ep', 'half'), 'tp'), parts along dimension 0, may hold values from -4 to 4
- cache_values: bfloat16 [512, 2, 64, 128], P(('groups', 'ep', 'half'), 'tp'), parts along dimension 0, may hold values from -4 to 4
- lengths: int32 [512], P(('groups', 'ep', 'half')), parts along dimension 0, may hold values from 1 to 64, as said below
- out_weight: bfloat16 [2048, 2048], P('tp', 'half'), may hold values from -0.375 to 0.375
- residual: bfloat16 [512, 2048], P(('groups', 'ep'), 'half'), parts along dimension 0, may hold values from -5 to 5
- norm_gain: float32 [2048], P('half'), may hold values from 0.1 to 1.9
- expert_ids: int32 [512, 8], P(('groups', 'ep')), parts along dimension 0, may hold values from 0 to 63, all different within a row; in each aligned block of 64 rows (0 to 63, 64 to 127, ...) at most 12 rows name the same one
- gate_weights: float32 [512, 8], P(('groups', 'ep')), parts along dimension 0, may hold values from 0.05 to 1
- w_gate: bfloat16 [64, 768, 2048], P(('ep', 'tp'), 'half'), may hold values from -0.125 to 0.125
- w_up: bfloat16 [64, 768, 2048], P(('ep', 'tp'), 'half'), may hold values from -0.125 to 0.125
- w_down: bfloat16 [64, 768, 2048], P(('ep', 'tp'), 'half'), may hold values from -0.625 to 0.625
Outputs:
- layer_out: bfloat16 [512, 2048], P(('groups', 'ep'), ('half', 'tp')), parts along dimension 0
There are 2 independent parts, one for each index of `groups`. A program takes and returns all parts, laid end to end along the dimension named above; an argument that names none is the same for every part. Nothing has to cross between parts.
Inputs may be any that keep to these rules, and one draw needn't show every extreme that they name: `expert_ids`: in each block of 64 consecutive rows (the tokens of one index of ep) no expert is named by more than 12 rows. `lengths`: among each device's 32 requests one has 64 cached tokens.
All inputs are finite; a program needn't handle non-finite values.
Results may differ from a plain program's by a relative error of at most 0.014.
Values may be sent and summed in bfloat16 or wider, within the bound.
A program may use at most 128 MiB of HBM per device.

v0:
```python
import math

import jax
import jax.numpy as jnp
from jax import lax
from jax.sharding import PartitionSpec as P

EXPERTS = 64


EPSILON = 1e-06


def attend(queries, new_keys, new_values, cache_keys, cache_values, lengths):
    requests, key_heads, context, head_size = cache_keys.shape
    sharing = queries.shape[1] // (key_heads * head_size)
    query_blocks = queries.reshape(requests, key_heads, sharing, head_size)
    score_scale = 1.0 / math.sqrt(head_size)
    scores = (
        jnp.einsum("rkgd,rkcd->rkgc", query_blocks, cache_keys, preferred_element_type=jnp.float32)
        * score_scale
    )
    own_score = (
        jnp.einsum(
            "rkgd,rkd->rkg",
            query_blocks,
            new_keys.reshape(requests, key_heads, head_size),
            preferred_element_type=jnp.float32,
        )
        * score_scale
    )
    valid = lax.iota(jnp.int32, context)[None, :] < lengths[:, None]
    scores = jnp.where(valid[:, None, None, :], scores, -1e30)
    highest = jnp.maximum(jnp.max(scores, axis=-1), own_score)
    weights = jnp.exp(scores - highest[..., None])
    own_weight = jnp.exp(own_score - highest)
    denominator = jnp.sum(weights, axis=-1) + own_weight
    probs = (weights / denominator[..., None]).astype(jnp.bfloat16)
    own_prob = (own_weight / denominator).astype(jnp.bfloat16)
    mixture = jnp.einsum("rkgc,rkcd->rkgd", probs, cache_values, preferred_element_type=jnp.float32)
    mixture = mixture + own_prob.astype(jnp.float32)[..., None] * new_values.reshape(
        requests, key_heads, 1, head_size
    ).astype(jnp.float32)
    return mixture.astype(jnp.bfloat16).reshape(requests, key_heads * sharing * head_size)


def combine_rows(returned_rows, target, gates):
    token_rows, top_count = target.shape
    safe_target = jnp.maximum(target, 0).reshape(-1)
    picked = jnp.take(returned_rows, safe_target, axis=0).reshape(
        token_rows, top_count, returned_rows.shape[1]
    )
    weighting = jnp.where(target >= 0, gates, 0.0)
    return jnp.sum(picked.astype(jnp.float32) * weighting[..., None], axis=1)


def on_device(
    queries,
    new_keys,
    new_values,
    cache_keys,
    cache_values,
    lengths,
    out_weight,
    residual,
    norm_gain,
    expert_ids,
    gate_weights,
    w_gate,
    w_up,
    w_down,
):
    attended = attend(queries, new_keys, new_values, cache_keys, cache_values, lengths)
    partial_mix = jnp.dot(
        lax.all_gather(attended, "half", axis=0, tiled=True),
        out_weight,
        preferred_element_type=jnp.float32,
    )
    mixed = lax.psum(partial_mix.astype(jnp.bfloat16), "tp").astype(jnp.float32)
    hidden = residual.astype(jnp.float32) + mixed
    squares = lax.psum(jnp.sum(hidden * hidden, axis=1), "half")
    half_width = hidden.shape[1]
    width = half_width * lax.axis_size("half")
    normed = (hidden * lax.rsqrt(squares / width + EPSILON)[:, None] * norm_gain[None, :]).astype(
        jnp.bfloat16
    )
    token_rows, top_count = expert_ids.shape
    ep_count = lax.axis_size("ep")
    tp_count = lax.axis_size("tp")
    local_experts = w_gate.shape[0]
    capacity = token_rows * top_count * 3 // (2 * EXPERTS)
    slot_count = ep_count * local_experts * capacity
    flat_ids = expert_ids.reshape(-1)
    one_hot = (flat_ids[:, None] == lax.iota(jnp.int32, EXPERTS)[None, :]).astype(jnp.int32)
    earlier = jnp.cumsum(one_hot, axis=0) - one_hot
    slot = jnp.sum(earlier * one_hot, axis=1)
    owner_ep = flat_ids // (local_experts * tp_count)
    owner_tp = flat_ids // local_experts % tp_count
    target = owner_ep * (local_experts * capacity) + flat_ids % local_experts * capacity + slot
    target = jnp.where(owner_tp == lax.axis_index("tp"), target, -1).reshape(token_rows, top_count)
    dispatch_matrix = jnp.any(
        lax.iota(jnp.int32, slot_count)[:, None, None] == target[None, :, :], axis=2
    ).astype(jnp.bfloat16)
    gates = gate_weights / jnp.sum(gate_weights, axis=1, keepdims=True)
    full_rows = lax.all_gather(normed, "half", axis=1, tiled=True)
    outgoing = jnp.dot(dispatch_matrix, full_rows, preferred_element_type=jnp.float32).astype(
        jnp.bfloat16
    )
    arrived = lax.all_to_all(
        outgoing.reshape(ep_count, local_experts, capacity, width),
        "ep",
        split_axis=0,
        concat_axis=0,
        tiled=True,
    )
    gate_part = jnp.einsum("secd,efd->secf", arrived, w_gate, preferred_element_type=jnp.float32)
    up_part = jnp.einsum("secd,efd->secf", arrived, w_up, preferred_element_type=jnp.float32)
    activation = (jax.nn.silu(gate_part) * up_part).astype(jnp.bfloat16)
    expert_out = jnp.einsum(
        "secf,efd->secd", activation, w_down, preferred_element_type=jnp.float32
    ).astype(jnp.bfloat16)
    summed = lax.psum_scatter(
        expert_out.astype(jnp.float32).astype(jnp.bfloat16), "half", scatter_dimension=3, tiled=True
    ).astype(jnp.float32)
    returned = lax.all_to_all(
        summed.reshape(ep_count, local_experts * capacity, half_width).astype(jnp.bfloat16),
        "ep",
        split_axis=0,
        concat_axis=0,
        tiled=True,
    ).astype(jnp.float32)
    term = combine_rows(returned.reshape(slot_count, half_width), target, gates)
    expert_sum = lax.psum_scatter(
        term.astype(jnp.bfloat16), "tp", scatter_dimension=1, tiled=True
    ).astype(jnp.float32)
    slice_width = expert_sum.shape[1]
    own_columns = lax.dynamic_slice_in_dim(
        hidden, lax.axis_index("tp") * slice_width, slice_width, 1
    )
    return (own_columns + expert_sum).astype(jnp.bfloat16)


def solution(mesh):
    placed = (
        P(("groups", "ep", "half"), "tp"),
        P(("groups", "ep", "half"), "tp"),
        P(("groups", "ep", "half"), "tp"),
        P(("groups", "ep", "half"), "tp", None, None),
        P(("groups", "ep", "half"), "tp", None, None),
        P(("groups", "ep", "half")),
        P("tp", "half"),
        P(("groups", "ep"), "half"),
        P("half"),
        P(("groups", "ep"), None),
        P(("groups", "ep"), None),
        P(("ep", "tp"), "half", None),
        P(("ep", "tp"), "half", None),
        P(("ep", "tp"), "half", None),
    )
    return jax.shard_map(
        on_device,
        mesh=mesh,
        in_specs=placed,
        out_specs=P(("groups", "ep"), ("half", "tp")),
        check_vma=False,
    )
```

profile of v0, /device:TPU:0, one launch (start us, length us, event | category | flops | bytes accessed | tf_op | source)
XLA Modules:
  0.0 210.5 jit_solution(17106588360139845303)
XLA Ops:
  6.5 1.0 copy.78
  7.5 0.7 iota_compare_fusion.3
  8.3 0.8 fusion.58
  9.1 1.5 fusion.76
  10.6 0.2 fusion.55
  10.9 0.7 convert_element_type.73
  11.6 1.4 fusion.41
  13.0 6.0 %all_gather.6 = bf16[64,1024]{1,0:T(8,128)(2,1)S(1)} all-gather(bf16[32,1024]{1,0:T(8,128)(2,1)S(1)} %bitcast.97), channel_id=1, replica_groups=mesh['groups'=2,'ep'=4,'half'=2,'tp'=2] {'half'}, dimensions={0}, use_global_device_ids=true | all-gather | bytes 196608 | tf_op jit(solution)/shard_map/all_gather | solution.py:75
  18.9 1.1 convolution_convert_fusion.1
  20.1 0.0 all-reduce.2.cloned.1.call-update
  20.1 0.0 reduce-scatter.3.cloned.1.call-start
  20.2 0.1 copy.59
  20.2 0.1 eq.56
  20.3 0.1 eq.52
  20.4 1.2 reduce-window.6
  21.7 0.2 slice_reduce_fusion
  21.9 0.1 fusion.53
  22.1 0.1 reduce_sum.49
  22.2 0.1 copy.62
  22.3 0.1 copy.64
  22.3 0.3 fusion.47
  22.6 17.3 %all-reduce.2.cloned.1.call-done = bf16[64,1024]{1,0:T(8,128)(2,1)} async-done(((bf16[64,1024]{1,0:T(8,128)(2,1)}), bf16[64,1024]{1,0:T(8,128)(2,1)}) %all-reduce.2.cloned.1.call-update) | async-done | bytes 131088 | tf_op jit(solution)/shard_map/psum | solution.py:79
  40.0 1.0 convert_add_fusion
  41.0 4.9 %psum.15 = f32[64]{0:T(128)S(1)} all-reduce(f32[64]{0:T(128)S(1)} %get-tuple-element.8), channel_id=1, replica_groups=mesh['groups'=2,'ep'=4,'half'=2,'tp'=2] {'half'}, use_global_device_ids=true, to_apply=%region_8.9 | all-reduce | flops 64 | bytes 512 | tf_op jit(solution)/shard_map/psum | solution.py:81
  46.0 1.0 multiply_convert_fusion
  47.0 5.6 %all_gather.7 = bf16[64,2048]{1,0:T(8,128)(2,1)S(1)} all-gather(bf16[64,1024]{1,0:T(8,128)(2,1)S(1)} %multiply_convert_fusion), channel_id=1, replica_groups=mesh['groups'=2,'ep'=4,'half'=2,'tp'=2] {'half'}, dimensions={1}, use_global_device_ids=true | all-gather | bytes 393216 | tf_op jit(solution)/shard_map/all_gather | solution.py:105
  52.6 1.8 convolution_convert_fusion
  54.4 3.6 %reshape.224 = bf16[4,8,12,2048]{3,2,1,0:T(8,128)(2,1)} reshape(bf16[384,2048]{1,0:T(8,128)(2,1)} %convolution_convert_fusion) | data formatting | bytes 3145728 | tf_op jit(solution)/shard_map/reshape | solution.py:110
  58.0 2.5 %copy.65 = bf16[4,8,12,2048]{3,1,2,0:T(8,128)(2,1)S(1)} copy(bf16[4,8,12,2048]{3,2,1,0:T(8,128)(2,1)} %reshape.224) | data formatting | bytes 3145728 | tf_op jit(solution)/shard_map/reshape | solution.py:110
  60.5 39.8 %all_to_all.10 = bf16[4,8,12,2048]{3,1,2,0:T(8,128)(2,1)S(1)} all-to-all(bf16[4,8,12,2048]{3,1,2,0:T(8,128)(2,1)S(1)} %copy.65), channel_id=1, replica_groups=mesh['groups'=2,'ep'=4,'half'=2,'tp'=2] {'ep'}, dimensions={0} | all-to-all | bytes 3145728 | tf_op jit(solution)/shard_map/all_to_all | solution.py:109
  100.3 1.1 copy-done.1
  101.4 8.7 %fusion.16 = f32[4,8,12,384]{3,2,0,1:T(8,128)S(1)} fusion(bf16[8,384,2048]{2,1,0:T(8,128)(2,1)} %param.25, bf16[4,8,12,2048]{3,1,2,0:T(8,128)(2,1)S(1)} %all_to_all.10), kind=kOutput, calls=%fused_computation.15 | convolution fusion | flops 603979776 | bytes 14745600 | tf_op jit(solution)/shard_map/secd,efd->secf/dot_general | solution.py:116
  110.1 18.4 %fusion.9 = bf16[4,8,12,2048]{3,2,0,1:T(8,128)(2,1)} fusion(bf16[8,384,2048]{2,1,0:T(8,128)(2,1)} %param.27, bf16[8,384,2048]{2,1,0:T(8,128)(2,1)} %param.26, bf16[4,8,12,2048]{3,1,2,0:T(8,128)(2,1)} %copy-done.1, f32[4,8,12,384]{3,2,0,1:T(8,128)S(1)} %fusion.16), kind=kOutput, calls=%fused_computation.9 | convolution fusion | flops 1209630720 | bytes 28901376 | tf_op jit(solution)/shard_map/secf,efd->secd/dot_general | solution.py:119
  128.5 0.0 reduce-scatter.3.cloned.1.call-update
  128.5 31.0 %reduce-scatter.3.cloned.1.call-done = bf16[4,8,12,1024]{3,2,0,1:T(8,128)(2,1)} async-done(((bf16[4,8,12,2048]{3,2,0,1:T(8,128)(2,1)}), bf16[4,8,12,1024]{3,2,0,1:T(8,128)(2,1)}) %reduce-scatter.3.cloned.1.call-update) | async-done | bytes 786448 | tf_op jit(solution)/shard_map/reduce_scatter | solution.py:122
  159.5 1.8 copy.68
  161.4 1.1 copy.69
  162.5 4.6 %all-to-all-start.1 = ((bf16[4,96,1024]{2,1,0:T(8,128)(2,1)}), bf16[4,96,1024]{2,1,0:T(8,128)(2,1)S(1)}, u32[]{:S(2)}, u32[]{:S(2)}) async-start(bf16[4,96,1024]{2,1,0:T(8,128)(2,1)} %copy.69), calls=%async_computation.2 | async-start | bytes 1572864 | tf_op jit(solution)/shard_map/all_to_all | solution.py:125
  167.1 0.1 copy.70
  167.2 0.1 reshape.227
  167.3 0.1 copy.71
  167.4 0.1 copy.63
  167.5 19.7 %all-to-all-done.1 = bf16[4,96,1024]{2,1,0:T(8,128)(2,1)S(1)} async-done(((bf16[4,96,1024]{2,1,0:T(8,128)(2,1)}), bf16[4,96,1024]{2,1,0:T(8,128)(2,1)S(1)}, u32[]{:S(2)}, u32[]{:S(2)}) %all-to-all-start.1) | async-done | bytes 786464 | tf_op jit(solution)/shard_map/all_to_all | solution.py:125
  187.2 1.4 bitcast_convert_fusion
  188.6 5.1 %gather_fusion = f32[512,1024]{1,0:T(8,128)} fusion(f32[384,1024]{1,0:T(8,128)} %bitcast_convert_fusion, s32[1024]{0:T(1024)S(1)} %pad_clamp_fusion), kind=kCustom, calls=%fused_computation | custom fusion | bytes 4196352 | tf_op jit(solution)/shard_map/jit(_take)/gather | solution.py:50
  193.6 3.0 %fusion.15 = bf16[64,1024]{1,0:T(8,128)(2,1)} fusion(f32[512,1024]{1,0:T(8,128)} %gather_fusion, f32[64,8]{1,0:T(8,128)S(1)} %copy.71, pred[64,8]{1,0:T(8,128)(4,1)S(1)} %copy.63), kind=kLoop, calls=%fused_computation.14 | loop fusion | flops 1507328 | bytes 2230784 | tf_op jit(solution)/shard_map/reduce_sum | solution.py:54
  196.7 5.8 %reduce-scatter.5.cloned.1.call-done = bf16[64,512]{1,0:T(8,128)(2,1)} async-done(((bf16[64,1024]{1,0:T(8,128)(2,1)}), bf16[64,512]{1,0:T(8,128)(2,1)}) %reduce-scatter.5.cloned.1.call-update) | async-done | bytes 65552 | tf_op jit(solution)/shard_map/reduce_scatter | solution.py:133
  202.5 1.5 add_convert_fusion
  (27 shorter events, 0.2 us)
Async XLA Ops:
  6.5 12.4 %copy-start = (bf16[1024,1024]{1,0:T(8,128)(2,1)S(1)}, bf16[1024,1024]{1,0:T(8,128)(2,1)}, u32[]{:S(2)}) copy-start(bf16[1024,1024]{1,0:T(8,128)(2,1)} %param.20) | copy-start | bytes 6291460
  6.5 33.4 %all-reduce.2.cloned.1.call-start = ((), (), s32[]{:S(2)}) async-start(), calls=%async_computation.4 | async-start | bytes 262144 | tf_op jit(solution)/shard_map/psum | solution.py:79
  10.6 9.5 %copy-start.3 = (s32[64,8]{0,1:T(8,128)S(1)}, s32[64,8]{0,1:T(8,128)}, u32[]{:S(2)}) copy-start(s32[64,8]{0,1:T(8,128)} %param.23) | copy-start | bytes 6148
  12.9 27.1 %copy-start.2 = (bf16[64,1024]{1,0:T(8,128)(2,1)S(1)}, bf16[64,1024]{1,0:T(8,128)(2,1)}, u32[]{:S(2)}) copy-start(bf16[64,1024]{1,0:T(8,128)(2,1)} %param.21) | copy-start | bytes 393220
  13.0 33.0 %copy-start.5 = (f32[1024]{0:T(1024)S(1)}, f32[1024]{0:T(1024)}, u32[]{:S(2)}) copy-start(f32[1024]{0:T(1024)} %param.22) | copy-start | bytes 12292
  20.1 139.4 %reduce-scatter.3.cloned.1.call-start = ((), (), s32[]{:S(2)}) async-start(), calls=%async_computation.5 | async-start | bytes 3145728 | tf_op jit(solution)/shard_map/reduce_scatter | solution.py:122
  100.3 1.1 copy-start.1
  128.5 38.8 %copy-start.4 = (f32[64,8]{0,1:T(8,128)S(1)}, f32[64,8]{0,1:T(8,128)}, u32[]{:S(2)}) copy-start(f32[64,8]{0,1:T(8,128)} %param.24) | copy-start | bytes 6148
  162.5 24.7 %all-to-all-start.1 = ((bf16[4,96,1024]{2,1,0:T(8,128)(2,1)}), bf16[4,96,1024]{2,1,0:T(8,128)(2,1)S(1)}, u32[]{:S(2)}, u32[]{:S(2)}) async-start(bf16[4,96,1024]{2,1,0:T(8,128)(2,1)} %copy.69), calls=%async_computation.2 | async-start | bytes 1572864 | tf_op jit(solution)/shard_map/all_to_all | solution.py:125
  167.1 35.4 %reduce-scatter.5.cloned.1.call-start = ((), (), s32[]{:S(2)}) async-start(), calls=%async_computation.6 | async-start | bytes 196608 | tf_op jit(solution)/shard_map/reduce_scatter | solution.py:133
Sparse Core Ops, SparseCore 0:
  20.2 19.7 all-reduce.1
  128.6 30.8 reduce-scatter.2
  196.8 5.6 reduce-scatter.4
where the time goes:
time: 211 us; the launch traced here: 210 us
  waiting for transfers between devices  73.9 us (35%)
  blocking collectives  56.3 us (27%)
  matrix products  33.7 us (16%)
  local copies, waits for them, and re-layouts  17.4 us (8%)
  between operations  13.3 us (6%)
  other arithmetic  11.3 us (5%)
  starting transfers between devices  4.65 us (2%)
    all_to_all x1, blocking collectives, on_device(): lax.all_to_all(outgoing.reshape(ep_count, local_experts, capacity, width)...  39.8 us
    reduce_scatter x1, waiting for transfers between devices, on_device(): lax.psum_scatter(expert_out.astype(jnp.float32).astype(jnp.bfloat16), 'ha...  31 us
    all_to_all x1, waiting for transfers between devices, on_device(): lax.all_to_all(summed.reshape(ep_count, local_experts * capacity, half_wi...  19.7 us
    dot_general x1, matrix products, on_device(): jnp.einsum('secf,efd->secd', activation, w_down, preferred_element_type=j...  18.4 us
    psum x1, waiting for transfers between devices, on_device(): mixed = lax.psum(partial_mix.astype(jnp.bfloat16), 'tp').astype(jnp.float32)  17.3 us
    dot_general x1, matrix products, on_device(): jnp.einsum('secd,efd->secf', arrived, w_gate, preferred_element_type=jnp....  8.69 us
    reshape x2, local copies, waits for them, and re-layouts, on_device(): outgoing.reshape(ep_count, local_experts, capacity, width)  6.06 us
    all_gather x1, blocking collectives, on_device(): lax.all_gather(attended, 'half', axis=0, tiled=True)  5.97 us
  transfers between devices with their start and end apart: 4, of which 4 were waited for; matrix products, arithmetic and copies ran while one was open for 1% of the time, Pallas kernels for 0%

commit v1 on v0

--- a/solution.py
+++ b/solution.py
@@ -1,8 +1,11 @@
+import functools
 import math
 
 import jax
 import jax.numpy as jnp
 from jax import lax
+from jax.experimental import pallas as pl
+from jax.experimental.pallas import tpu as pltpu
 from jax.sharding import PartitionSpec as P
 
 EXPERTS = 64
@@ -54,7 +57,7 @@
     return jnp.sum(picked.astype(jnp.float32) * weighting[..., None], axis=1)
 
 
-def on_device(
+def staged(
     queries,
     new_keys,
     new_values,
@@ -140,6 +143,503 @@
     return (own_columns + expert_sum).astype(jnp.bfloat16)
 
 
+VMEM_BYTES = 60 * 1024 * 1024
+LANES = 128
+ROW_TILE = 8
+MESH = pl.DeviceIdType.MESH
+
+
+def remote(src, dst, send, recv, **where):
+    return pltpu.make_async_remote_copy(
+        src_ref=src,
+        dst_ref=dst,
+        send_sem=send,
+        recv_sem=recv,
+        device_id=where,
+        device_id_type=MESH,
+    )
+
+
+def layer_kernel(
+    sizes,
+    q_ref,
+    nk_ref,
+    nv_ref,
+    len_ref,
+    res_ref,
+    gain_ref,
+    ids_ref,
+    gw_ref,
+    ck_hbm,
+    cv_hbm,
+    ow_hbm,
+    wg_hbm,
+    wu_hbm,
+    wd_hbm,
+    out_ref,
+    ck,
+    cv,
+    ow,
+    wg,
+    wu,
+    wd,
+    att_f,
+    att,
+    gain,
+    table,
+    mix_out,
+    mix_in,
+    own_hidden,
+    hid,
+    xg,
+    squares,
+    act,
+    a_out,
+    a_in,
+    mine,
+    b_out,
+    b_in,
+    kept,
+    c_out,
+    c_in,
+    load_sem,
+    w_sem,
+    att_s,
+    att_r,
+    gain_s,
+    gain_r,
+    table_s,
+    table_r,
+    mix_s,
+    mix_r,
+    hz_s,
+    hz_r,
+    hx_s,
+    hx_r,
+    ht_s,
+    ht_r,
+    a_s,
+    a_r,
+    b_s,
+    b_r,
+    c_s,
+    c_r,
+):
+    n_ep, n_half = sizes["ep"], sizes["half"]
+    me_z, me_h, me_t = lax.axis_index("ep"), lax.axis_index("half"), lax.axis_index("tp")
+    other = 1 - me_t
+    requests, context, head_size = ck.shape
+    heads = q_ref.shape[1] // head_size
+    local, hidden_units = wg.shape[0], wg.shape[1]
+    block, piece = res_ref.shape[0], res_ref.shape[1] // 2
+    rows = n_ep * block
+    width = n_half * 2 * piece
+
+    loads = [
+        pltpu.make_async_copy(ck_hbm, ck, load_sem.at[0]),
+        pltpu.make_async_copy(cv_hbm, cv, load_sem.at[1]),
+        pltpu.make_async_copy(ow_hbm, ow, load_sem.at[2]),
+    ]
+    for load in loads:
+        load.start()
+
+    def weight_copy(k, j):
+        if k < 2:
+            return pltpu.make_async_copy(
+                (wg_hbm, wu_hbm)[k].at[j], (wg, wu)[k].at[j], w_sem.at[k, j]
+            )
+        part = pl.ds(j * hidden_units, hidden_units)
+        return pltpu.make_async_copy(wd_hbm.at[part], wd.at[part], w_sem.at[k, j])
+
+    for j in range(local):
+        weight_copy(0, j).start()
+        weight_copy(1, j).start()
+    for j in range(local):
+        weight_copy(2, j).start()
+
+    barrier = pltpu.get_barrier_semaphore()
+    pl.semaphore_signal(barrier, inc=1, device_id={"tp": other}, device_id_type=MESH)
+    for d in range(1, n_half):
+        pl.semaphore_signal(
+            barrier, inc=1, device_id={"half": lax.rem(me_h + d, n_half)}, device_id_type=MESH
+        )
+    for d in range(1, n_ep):
+        pl.semaphore_signal(
+            barrier, inc=1, device_id={"ep": lax.rem(me_z + d, n_ep)}, device_id_type=MESH
+        )
+
+    sent = []
+
+    def go(copy):
+        copy.start()
+        sent.append(copy)
+        return copy
+
+    gates = gw_ref[...] / jnp.sum(gw_ref[...], axis=1, keepdims=True)
+    expert_lane = lax.broadcasted_iota(jnp.int32, (block, table.shape[2]), 1)
+    own_table = jnp.zeros((block, table.shape[2]), jnp.float32)
+    for k in range(ids_ref.shape[1]):
+        own_table += jnp.where(expert_lane == ids_ref[:, k : k + 1], gates[:, k : k + 1], 0.0)
+    table[me_z] = own_table
+    gain[me_h] = jnp.broadcast_to(gain_ref[...], gain.shape[1:])
+
+    pl.semaphore_wait(barrier, 1 + (n_half - 1) + (n_ep - 1))
+
+    gain_copies = [
+        go(
+            remote(
+                gain.at[me_h],
+                gain.at[me_h],
+                gain_s.at[d],
+                gain_r.at[d],
+                half=lax.rem(me_h + d, n_half),
+            )
+        )
+        for d in range(1, n_half)
+    ]
+    table_copies = [
+        go(
+            remote(
+                table.at[me_z],
+                table.at[me_z],
+                table_s.at[d],
+                table_r.at[d],
+                ep=lax.rem(me_z + d, n_ep),
+            )
+        )
+        for d in range(1, n_ep)
+    ]
+
+    loads[0].wait()
+    loads[1].wait()
+    step = ROW_TILE
+    scale = 1.0 / math.sqrt(head_size)
+    shape = (heads * step, step * context)
+    row = lax.broadcasted_iota(jnp.int32, shape, 0)
+    column = lax.broadcasted_iota(jnp.int32, shape, 1)
+    same = (row % step) == (column // context)
+    position = column % context
+    for g in range(requests // step):
+        part = pl.ds(g * step, step)
+        q_all = q_ref[part].astype(jnp.float32)
+        q = jnp.concatenate(
+            [q_all[:, h * head_size : (h + 1) * head_size] for h in range(heads)], axis=0
+        )
+        nk = jnp.concatenate([nk_ref[part].astype(jnp.float32)] * heads, axis=0)
+        nv = jnp.concatenate([nv_ref[part].astype(jnp.float32)] * heads, axis=0)
+        valid = jnp.concatenate([len_ref[part]] * heads, axis=0)
+        keys = ck[part].reshape(step * context, head_size)
+        values = cv[part].reshape(step * context, head_size)
+        scores = (
+            lax.dot_general(
+                q.astype(jnp.bfloat16),
+                keys,
+                (((1,), (1,)), ((), ())),
+                preferred_element_type=jnp.float32,
+            )
+            * scale
+        )
+        own = jnp.sum(q * nk, axis=1, keepdims=True) * scale
+        scores = jnp.where(same & (position < valid), scores, -1e30)
+        highest = jnp.maximum(jnp.max(scores, axis=1, keepdims=True), own)
+        weights = jnp.exp(scores - highest)
+        own_weight = jnp.exp(own - highest)
+        inverse = 1.0 / (jnp.sum(weights, axis=1, keepdims=True) + own_weight)
+        probs = (weights * inverse).astype(jnp.bfloat16)
+        own_prob = (own_weight * inverse).astype(jnp.bfloat16).astype(jnp.float32)
+        mixture = jnp.dot(probs, values, preferred_element_type=jnp.float32) + own_prob * nv
+        for h in range(heads):
+            att_f[part, h * head_size : (h + 1) * head_size] = mixture[h * step : (h + 1) * step]
+    att[me_h] = att_f[...].astype(jnp.bfloat16)
+    att_copies = [
+        go(
+            remote(
+                att.at[me_h],
+                att.at[me_h],
+                att_s.at[d],
+                att_r.at[d],
+                half=lax.rem(me_h + d, n_half),
+            )
+        )
+        for d in range(1, n_half)
+    ]
+    loads[2].wait()
+    for copy in att_copies:
+        copy.wait_recv()
+
+    attended = att[...].reshape(block, att.shape[2])
+    other_columns = pl.ds(pl.multiple_of(other * piece, piece), piece)
+    my_columns = pl.ds(pl.multiple_of(me_t * piece, piece), piece)
+    mix_out[...] = jnp.dot(
+        attended, ow[:, other_columns], preferred_element_type=jnp.float32
+    ).astype(jnp.bfloat16)
+    mix_copy = go(remote(mix_out, mix_in, mix_s, mix_r, tp=other))
+    mixed = jnp.dot(attended, ow[:, my_columns], preferred_element_type=jnp.float32)
+    mixed = mixed + res_ref[:, my_columns].astype(jnp.float32)
+    mix_copy.wait_recv()
+    hidden = mixed + mix_in[...].astype(jnp.float32)
+    own_hidden[...] = hidden
+    hid[me_z, me_h, me_t] = hidden.astype(jnp.bfloat16)
+
+    z_copies = {
+        d: go(
+            remote(
+                hid.at[me_z, me_h, me_t],
+                hid.at[me_z, me_h, me_t],
+                hz_s.at[d],
+                hz_r.at[d],
+                ep=lax.rem(me_z + d, n_ep),
+            )
+        )
+        for d in range(1, n_ep)
+    }
+    for copy in gain_copies:
+        copy.wait_recv()
+    squares[...] = jnp.zeros_like(squares)
+
+    def take(z, h, t):
+        value = hid[z, h, t].astype(jnp.float32)
+        square = value * value
+        total = square[:, :LANES]
+        for k in range(1, piece // LANES):
+            total = total + square[:, k * LANES : (k + 1) * LANES]
+        squares[z] += total
+        columns = pl.ds(pl.multiple_of((h * 2 + t) * piece, piece), piece)
+        gain_columns = pl.ds(pl.multiple_of(t * piece, piece), piece)
+        xg[pl.ds(pl.multiple_of(z * block, block), block), columns] = (
+            value * gain[h, 0:1, gain_columns]
+        ).astype(jnp.bfloat16)
+
+    x_copies, t_copies = {}, {}
+    for d in range(n_ep):
+        z = lax.rem(me_z - d + n_ep, n_ep)
+        if d > 0:
+            z_copies[d].wait_recv()
+        here = hid.at[z, me_h, me_t]
+        for dx in range(1, n_half):
+            x_copies[d, dx] = go(
+                remote(
+                    here,
+                    here,
+                    hx_s.at[dx, d],
+                    hx_r.at[dx, d],
+                    half=lax.rem(me_h + dx, n_half),
+                )
+            )
+        t_copies[d, 0] = go(remote(here, here, ht_s.at[0, d], ht_r.at[0, d], tp=other))
+        take(z, me_h, me_t)
+    for d in range(n_ep):
+        z = lax.rem(me_z - d + n_ep, n_ep)
+        for dx in range(1, n_half):
+            h = lax.rem(me_h - dx + n_half, n_half)
+            x_copies[d, dx].wait_recv()
+            here = hid.at[z, h, me_t]
+            t_copies[d, dx] = go(remote(here, here, ht_s.at[dx, d], ht_r.at[dx, d], tp=other))
+            take(z, h, me_t)
+    for dx in range(n_half):
+        for d in range(n_ep):
+            z = lax.rem(me_z - d + n_ep, n_ep)
+            h = lax.rem(me_h - dx + n_half, n_half)
+            t_copies[d, dx].wait_recv()
+            take(z, h, other)
+    for copy in table_copies:
+        copy.wait_recv()
+
+    total = jnp.sum(squares[...].reshape(rows, LANES), axis=1, keepdims=True)
+    inverse = lax.rsqrt(total / width + EPSILON)
+    lane = lax.broadcasted_iota(jnp.int32, (rows, table.shape[2]), 1)
+    first = (me_z * 2 + me_t) * local
+
+    def expert(j, carry):
+        weight_copy(0, j).wait()
+        weight_copy(1, j).wait()
+        normed = xg[...]
+        contract = (((1,), (1,)), ((), ()))
+        gate = lax.dot_general(normed, wg[j], contract, preferred_element_type=jnp.float32)
+        up = lax.dot_general(normed, wu[j], contract, preferred_element_type=jnp.float32)
+        weight = jnp.sum(
+            jnp.where(lane == first + j, table[...].reshape(rows, table.shape[2]), 0.0),
+            axis=1,
+            keepdims=True,
+        )
+        gate = gate * inverse
+        silu = gate / (1.0 + jnp.exp(jnp.minimum(-gate, 88.0)))
+        act[:, pl.ds(pl.multiple_of(j * hidden_units, hidden_units), hidden_units)] = (
+            silu * (up * (inverse * weight))
+        ).astype(jnp.bfloat16)
+        return carry
+
+    lax.fori_loop(0, local, expert, 0)
+    for j in range(local):
+        weight_copy(2, j).wait()
+
+    def down(h, t):
+        columns = pl.ds(pl.multiple_of((h * 2 + t) * piece, piece), piece)
+        return jnp.dot(act[...], wd[:, columns], preferred_element_type=jnp.float32)
+
+    b_copies = {}
+    for dx in [*range(1, n_half), 0]:
+        h = lax.rem(me_h + dx, n_half)
+        a_out[dx] = down(h, other).astype(jnp.bfloat16)
+        a_copy = go(remote(a_out.at[dx], a_in.at[dx], a_s.at[dx], a_r.at[dx], tp=other))
+        mine[...] = down(h, me_t)
+        a_copy.wait_recv()
+        if dx > 0:
+            b_out[dx] = (mine[...] + a_in[dx].astype(jnp.float32)).astype(jnp.bfloat16)
+            for d in [*range(1, n_ep), 0]:
+                z = lax.rem(me_z + d, n_ep)
+                part = pl.ds(pl.multiple_of(z * block, block), block)
+                b_copies[dx, d] = go(
+                    remote(
+                        b_out.at[dx, part],
+                        b_in.at[dx, part],
+                        b_s.at[dx, d],
+                        b_r.at[dx, d],
+                        half=h,
+                    )
+                )
+        else:
+            kept[...] = mine[...] + a_in[dx].astype(jnp.float32)
+    c_copies = {}
+    for d in [*range(1, n_ep), 0]:
+        z = lax.rem(me_z + d, n_ep)
+        part = pl.ds(pl.multiple_of(z * block, block), block)
+        total = kept[part]
+        for dx in range(1, n_half):
+            b_copies[dx, d].wait_recv()
+            total = total + b_in[dx, part].astype(jnp.float32)
+        if d > 0:
+            c_out[d] = total.astype(jnp.bfloat16)
+            c_copies[d] = go(remote(c_out.at[d], c_in.at[d], c_s.at[d], c_r.at[d], ep=z))
+        else:
+            own_hidden[...] += total
+    result = own_hidden[...]
+    for d in range(1, n_ep):
+        c_copies[d].wait_recv()
+        result = result + c_in[d].astype(jnp.float32)
+    out_ref[...] = result.astype(jnp.bfloat16)
+    for copy in sent:
+        copy.wait_send()
+
+
+def on_device(sizes, *args):
+    (
+        queries,
+        new_keys,
+        new_values,
+        cache_keys,
+        cache_values,
+        lengths,
+        out_weight,
+        residual,
+        norm_gain,
+        expert_ids,
+        gate_weights,
+        w_gate,
+        w_up,
+        w_down,
+    ) = args
+    n_ep, n_half, n_tp = sizes["ep"], sizes["half"], sizes["tp"]
+    requests, key_heads, context, head_size = cache_keys.shape
+    block, half_width = residual.shape
+    local, hidden_units, width = w_gate.shape
+    piece = half_width // 2
+    rows = n_ep * block
+    lanes = -(-(local * n_ep * n_tp) // LANES) * LANES
+    bf16, f32 = jnp.bfloat16, jnp.float32
+    buffers = [
+        ((requests, context, head_size), bf16),
+        ((requests, context, head_size), bf16),
+        (out_weight.shape, bf16),
+        (w_gate.shape, bf16),
+        (w_up.shape, bf16),
+        ((local * hidden_units, width), bf16),
+        (queries.shape, f32),
+        ((n_half,) + queries.shape, bf16),
+        ((n_half, ROW_TILE, half_width), f32),
+        ((n_ep, block, lanes), f32),
+        ((block, piece), bf16),
+        ((block, piece), bf16),
+        ((block, piece), f32),
+        ((n_ep, n_half, n_tp, block, piece), bf16),
+        ((rows, width), bf16),
+        ((n_ep, block, LANES), f32),
+        ((rows, local * hidden_units), bf16),
+        ((n_half, rows, piece), bf16),
+        ((n_half, rows, piece), bf16),
+        ((rows, piece), f32),
+        ((n_half, rows, piece), bf16),
+        ((n_half, rows, piece), bf16),
+        ((rows, piece), f32),
+        ((n_ep, block, piece), bf16),
+        ((n_ep, block, piece), bf16),
+    ]
+    held = sum(math.prod(shape) * jnp.dtype(kind).itemsize for shape, kind in buffers)
+    fits = (
+        held * 5 // 4 < VMEM_BYTES
+        and n_tp == 2
+        and key_heads == 1
+        and hidden_units % LANES == 0
+        and piece % LANES == 0
+        and requests % (2 * ROW_TILE) == 0
+        and block == n_half * requests
+    )
+    if not fits:
+        return staged(*args)
+    dma = pltpu.SemaphoreType.DMA
+    semaphores = [
+        dma((3,)),
+        dma((3, local)),
+        dma((n_half,)),
+        dma((n_half,)),
+        dma((n_half,)),
+        dma((n_half,)),
+        dma((n_ep,)),
+        dma((n_ep,)),
+        dma,
+        dma,
+        dma((n_ep,)),
+        dma((n_ep,)),
+        dma((n_half, n_ep)),
+        dma((n_half, n_ep)),
+        dma((n_half, n_ep)),
+        dma((n_half, n_ep)),
+        dma((n_half,)),
+        dma((n_half,)),
+        dma((n_half, n_ep)),
+        dma((n_half, n_ep)),
+        dma((n_ep,)),
+        dma((n_ep,)),
+    ]
+    vmem = pl.BlockSpec(memory_space=pltpu.VMEM)
+    hbm = pl.BlockSpec(memory_space=pl.ANY)
+    return pl.pallas_call(
+        functools.partial(layer_kernel, dict(ep=n_ep, half=n_half)),
+        out_shape=jax.ShapeDtypeStruct((block, piece), bf16),
+        in_specs=[vmem] * 8 + [hbm] * 6,
+        out_specs=vmem,
+        scratch_shapes=[pltpu.VMEM(shape, kind) for shape, kind in buffers] + semaphores,
+        compiler_params=pltpu.CompilerParams(
+            collective_id=0, has_side_effects=True, vmem_limit_bytes=VMEM_BYTES
+        ),
+    )(
+        queries,
+        new_keys,
+        new_values,
+        lengths.reshape(requests, 1),
+        residual,
+        norm_gain.reshape(1, half_width),
+        expert_ids,
+        gate_weights,
+        cache_keys.reshape(requests, context, head_size),
+        cache_values.reshape(requests, context, head_size),
+        out_weight,
+        w_gate,
+        w_up,
+        w_down.reshape(local * hidden_units, width),
+    )
+
+
 def solution(mesh):
     placed = (
         P(("groups", "ep", "half"), "tp"),
@@ -158,7 +658,7 @@
         P(("ep", "tp"), "half", None),
     )
     return jax.shard_map(
-        on_device,
+        functools.partial(on_device, mesh.shape),
         mesh=mesh,
         in_specs=placed,
         out_specs=P(("groups", "ep"), ("half", "tp")),

time: 211 us -> 64.5 us (0.31)
  waiting for transfers between devices: 73.9 us -> 0 us
  Pallas kernels: 0 us -> 58.7 us
  blocking collectives: 56.3 us -> 0 us
  matrix products: 33.7 us -> 0 us
  between operations: 13.3 us -> 0.01 us
  local copies, waits for them, and re-layouts: 17.4 us -> 5.56 us
  other arithmetic: 11.3 us -> 0 us
  starting transfers between devices: 4.65 us -> 0 us
    pallas_call x0 -> x1, Pallas kernels: none -> 58.7 us  [on_device(): pl.pallas_call(functools.partial(layer_kernel, dict(ep=n_ep, half=n_half)...]
    all_to_all x1 -> x0, blocking collectives: 39.8 us -> none  [on_device(): lax.all_to_all(outgoing.reshape(ep_count, local_experts, capacity, width)...]
    reduce_scatter x2 -> x0, waiting for transfers between devices: 36.8 us -> none  [the longest x1 31 us: on_device(): lax.psum_scatter(expert_out.astype(jnp.float32).astype(jnp.bfloat16), 'ha...]
    dot_general x7 -> x0, matrix products: 33.7 us -> none  [the longest x1 18.4 us: on_device(): jnp.einsum('secf,efd->secd', activation, w_down, preferred_element_type=j...]
    all_to_all x1 -> x0, waiting for transfers between devices: 19.7 us -> none  [on_device(): lax.all_to_all(summed.reshape(ep_count, local_experts * capacity, half_wi...]
    psum x1 -> x0, waiting for transfers between devices: 17.3 us -> none  [on_device(): mixed = lax.psum(partial_mix.astype(jnp.bfloat16), 'tp').astype(jnp.float32)]
    all_gather x2 -> x0, blocking collectives: 11.6 us -> none  [the longest x1 5.97 us: on_device(): lax.all_gather(attended, 'half', axis=0, tiled=True)]
    gather x1 -> x0, local copies, waits for them, and re-layouts: 5.07 us -> none  [combine_rows(): jnp.take(returned_rows, safe_target, axis=0)]
  transfers between devices with their start and end apart: 4 -> 0, of which waited for: 4 -> 0; matrix products, arithmetic and copies ran while one was open for 1% -> 0% of each run, Pallas kernels for 0% -> 0%
where the time goes in v1:
time: 64.5 us; the launch traced here: 64.3 us
  Pallas kernels  58.7 us (91%)
  local copies, waits for them, and re-layouts  5.56 us (9%)
    pallas_call x1, Pallas kernels, on_device(): pl.pallas_call(functools.partial(layer_kernel, dict(ep=n_ep, half=n_half)...  58.7 us
    unnamed x3, local copies, waits for them, and re-layouts  4.22 us
    reshape x1, local copies, waits for them, and re-layouts, on_device(): lengths.reshape(requests, 1)  1.33 us

profile of v1, /device:TPU:0, one launch (start us, length us, event | category | flops | bytes accessed | tf_op | source)
XLA Modules:
  0.0 64.3 jit_solution(14900304017748860958)
XLA Ops:
  0.0 1.3 %copy.15.len_ref = s32[32,1]{1,0:T(8,128)} copy(s32[32,1]{0,1:T(1,128)} %bitcast.9) | data formatting | bytes 256 | tf_op jit(solution)/shard_map/reshape | solution.py:629
  1.3 1.4 %copy.16.ids_ref = s32[64,8]{1,0:T(8,128)} copy(s32[64,8]{0,1:T(8,128)} %param.23) | data formatting | bytes 4096 | tf_op args[9]
  2.7 1.4 %copy.17.gw_ref = f32[64,8]{1,0:T(8,128)} copy(f32[64,8]{0,1:T(8,128)} %param.24) | data formatting | bytes 4096 | tf_op args[10]
  4.1 58.7 %shard_map.136 = bf16[64,512]{1,0:T(8,128)(2,1)} custom-call(bf16[32,1024]{1,0:T(8,128)(2,1)} %q_ref.1, bf16[32,128]{1,0:T(8,128)(2,1)} %nk_ref.1, bf16[32,128]{1,0:T(8,128)(2,1)} %nv_ref.1, s32[32,1]{1,0:T(8,128)} %copy.15.len_ref, bf16[64,1024]{1,0:T(8,128)(2,1)} %res_ref.1, f32[1,1024]{1,0:T(1,128)} %bitcast.8, s32[64,8]{1,0:T(8,128)} %copy.16.ids_ref, ...), custom_call_target="tpu_custom_call" | custom-call | tf_op jit(solution)/shard_map/pallas_call | solution.py:616
  62.8 1.5 %copy.19 = bf16[64,512]{1,0:T(8,128)(2,1)} copy(bf16[64,512]{1,0:T(8,128)(2,1)} %shard_map.136) | data formatting | bytes 131072

commit v2 on v1

--- a/solution.py
+++ b/solution.py
@@ -160,6 +160,19 @@
     )
 
 
+def partner(index, p):
+    bit = 1
+    while bit <= p:
+        if p & bit:
+            index = index + bit - 2 * bit * (index // bit % 2)
+        bit *= 2
+    return index
+
+
+def span_of(span):
+    return pl.ds(span.start, span.stop - span.start)
+
+
 def layer_kernel(
     sizes,
     q_ref,
@@ -180,8 +193,7 @@
     ck,
     cv,
     ow,
-    wg,
-    wu,
+    wgu,
     wd,
     att_f,
     att,
@@ -196,7 +208,6 @@
     act,
     a_out,
     a_in,
-    mine,
     b_out,
     b_in,
     kept,
@@ -230,7 +241,7 @@
     other = 1 - me_t
     requests, context, head_size = ck.shape
     heads = q_ref.shape[1] // head_size
-    local, hidden_units = wg.shape[0], wg.shape[1]
+    local, hidden_units = wgu.shape[0], wgu.shape[1] // 2
     block, piece = res_ref.shape[0], res_ref.shape[1] // 2
     rows = n_ep * block
     width = n_half * 2 * piece
@@ -246,7 +257,9 @@
     def weight_copy(k, j):
         if k < 2:
             return pltpu.make_async_copy(
-                (wg_hbm, wu_hbm)[k].at[j], (wg, wu)[k].at[j], w_sem.at[k, j]
+                (wg_hbm, wu_hbm)[k].at[j],
+                wgu.at[j, pl.ds(k * hidden_units, hidden_units)],
+                w_sem.at[k, j],
             )
         part = pl.ds(j * hidden_units, hidden_units)
         return pltpu.make_async_copy(wd_hbm.at[part], wd.at[part], w_sem.at[k, j])
@@ -263,10 +276,8 @@
         pl.semaphore_signal(
             barrier, inc=1, device_id={"half": lax.rem(me_h + d, n_half)}, device_id_type=MESH
         )
-    for d in range(1, n_ep):
-        pl.semaphore_signal(
-            barrier, inc=1, device_id={"ep": lax.rem(me_z + d, n_ep)}, device_id_type=MESH
-        )
+    for p in range(1, n_ep):
+        pl.semaphore_signal(barrier, inc=1, device_id={"ep": partner(me_z, p)}, device_id_type=MESH)
 
     sent = []
 
@@ -275,40 +286,7 @@
         sent.append(copy)
         return copy
 
-    gates = gw_ref[...] / jnp.sum(gw_ref[...], axis=1, keepdims=True)
-    expert_lane = lax.broadcasted_iota(jnp.int32, (block, table.shape[2]), 1)
-    own_table = jnp.zeros((block, table.shape[2]), jnp.float32)
-    for k in range(ids_ref.shape[1]):
-        own_table += jnp.where(expert_lane == ids_ref[:, k : k + 1], gates[:, k : k + 1], 0.0)
-    table[me_z] = own_table
-    gain[me_h] = jnp.broadcast_to(gain_ref[...], gain.shape[1:])
-
-    pl.semaphore_wait(barrier, 1 + (n_half - 1) + (n_ep - 1))
-
-    gain_copies = [
-        go(
-            remote(
-                gain.at[me_h],
-                gain.at[me_h],
-                gain_s.at[d],
-                gain_r.at[d],
-                half=lax.rem(me_h + d, n_half),
-            )
-        )
-        for d in range(1, n_half)
-    ]
-    table_copies = [
-        go(
-            remote(
-                table.at[me_z],
-                table.at[me_z],
-                table_s.at[d],
-                table_r.at[d],
-                ep=lax.rem(me_z + d, n_ep),
-            )
-        )
-        for d in range(1, n_ep)
-    ]
+    spread = jnp.broadcast_to(len_ref[...].astype(jnp.float32), (LANES, requests)).T
 
     loads[0].wait()
     loads[1].wait()
@@ -318,7 +296,7 @@
     row = lax.broadcasted_iota(jnp.int32, shape, 0)
     column = lax.broadcasted_iota(jnp.int32, shape, 1)
     same = (row % step) == (column // context)
-    position = column % context
+    position = (column % context).astype(jnp.float32)
     for g in range(requests // step):
         part = pl.ds(g * step, step)
         q_all = q_ref[part].astype(jnp.float32)
@@ -327,7 +305,7 @@
         )
         nk = jnp.concatenate([nk_ref[part].astype(jnp.float32)] * heads, axis=0)
         nv = jnp.concatenate([nv_ref[part].astype(jnp.float32)] * heads, axis=0)
-        valid = jnp.concatenate([len_ref[part]] * heads, axis=0)
+        valid = jnp.concatenate([spread[g * step : (g + 1) * step, :1]] * heads, axis=0)
         keys = ck[part].reshape(step * context, head_size)
         values = cv[part].reshape(step * context, head_size)
         scores = (
@@ -351,6 +329,15 @@
         for h in range(heads):
             att_f[part, h * head_size : (h + 1) * head_size] = mixture[h * step : (h + 1) * step]
     att[me_h] = att_f[...].astype(jnp.bfloat16)
+    gates = gw_ref[...] / jnp.sum(gw_ref[...], axis=0, keepdims=True)
+    expert_row = lax.broadcasted_iota(jnp.int32, (table.shape[2], block), 0)
+    own_table = jnp.zeros((table.shape[2], block), jnp.float32)
+    for k in range(ids_ref.shape[0]):
+        own_table += jnp.where(expert_row == ids_ref[k : k + 1, :], gates[k : k + 1, :], 0.0)
+    table[0] = own_table.T
+    gain[me_h] = jnp.broadcast_to(gain_ref[...], gain.shape[1:])
+
+    pl.semaphore_wait(barrier, 1 + (n_half - 1) + (n_ep - 1))
     att_copies = [
         go(
             remote(
@@ -362,6 +349,26 @@
             )
         )
         for d in range(1, n_half)
+    ]
+    gain_copies = [
+        go(
+            remote(
+                gain.at[me_h],
+                gain.at[me_h],
+                gain_s.at[d],
+                gain_r.at[d],
+                half=lax.rem(me_h + d, n_half),
+            )
+        )
+        for d in range(1, n_half)
+    ]
+    table_copies = [
+        go(
+            remote(
+                table.at[0], table.at[p], table_s.at[p], table_r.at[p], ep=partner(me_z, p)
+            )
+        )
+        for p in range(1, n_ep)
     ]
     loads[2].wait()
     for copy in att_copies:
@@ -379,144 +386,194 @@
     mix_copy.wait_recv()
     hidden = mixed + mix_in[...].astype(jnp.float32)
     own_hidden[...] = hidden
-    hid[me_z, me_h, me_t] = hidden.astype(jnp.bfloat16)
+    hid[0, me_h, me_t] = hidden.astype(jnp.bfloat16)
 
     z_copies = {
-        d: go(
+        p: go(
             remote(
-                hid.at[me_z, me_h, me_t],
-                hid.at[me_z, me_h, me_t],
-                hz_s.at[d],
-                hz_r.at[d],
-                ep=lax.rem(me_z + d, n_ep),
-            )
-        )
-        for d in range(1, n_ep)
+                hid.at[0, me_h, me_t],
+                hid.at[p, me_h, me_t],
+                hz_s.at[p],
+                hz_r.at[p],
+                ep=partner(me_z, p),
+            )
+        )
+        for p in range(1, n_ep)
     }
-    for copy in gain_copies:
-        copy.wait_recv()
-    squares[...] = jnp.zeros_like(squares)
-
-    def take(z, h, t):
-        value = hid[z, h, t].astype(jnp.float32)
+    x_copies, t_copies = {}, {}
+
+    def take(p, h, t):
+        value = hid[p, h, t].astype(jnp.float32)
         square = value * value
         total = square[:, :LANES]
         for k in range(1, piece // LANES):
             total = total + square[:, k * LANES : (k + 1) * LANES]
-        squares[z] += total
+        squares[p] += total
         columns = pl.ds(pl.multiple_of((h * 2 + t) * piece, piece), piece)
         gain_columns = pl.ds(pl.multiple_of(t * piece, piece), piece)
-        xg[pl.ds(pl.multiple_of(z * block, block), block), columns] = (
-            value * gain[h, 0:1, gain_columns]
-        ).astype(jnp.bfloat16)
-
-    x_copies, t_copies = {}, {}
-    for d in range(n_ep):
-        z = lax.rem(me_z - d + n_ep, n_ep)
-        if d > 0:
-            z_copies[d].wait_recv()
-        here = hid.at[z, me_h, me_t]
-        for dx in range(1, n_half):
-            x_copies[d, dx] = go(
+        xg[p * block : (p + 1) * block, columns] = (value * gain[h, 0:1, gain_columns]).astype(
+            jnp.bfloat16
+        )
+
+    def to_sibling(p, dx, h):
+        here = hid.at[p, h, me_t]
+        t_copies[p, dx] = go(remote(here, here, ht_s.at[dx, p], ht_r.at[dx, p], tp=other))
+
+    def spread_own(group):
+        for p in group:
+            if p > 0:
+                z_copies[p].wait_recv()
+            here = hid.at[p, me_h, me_t]
+            for dx in range(1, n_half):
+                x_copies[p, dx] = go(
+                    remote(
+                        here,
+                        here,
+                        hx_s.at[dx, p],
+                        hx_r.at[dx, p],
+                        half=lax.rem(me_h + dx, n_half),
+                    )
+                )
+            to_sibling(p, 0, me_h)
+
+    def spread_crossed(group):
+        for p in group:
+            for dx in range(1, n_half):
+                x_copies[p, dx].wait_recv()
+                to_sibling(p, dx, lax.rem(me_h - dx + n_half, n_half))
+
+    def take_all(group):
+        for dx in range(n_half):
+            for p in group:
+                h = lax.rem(me_h - dx + n_half, n_half)
+                take(p, h, me_t)
+                t_copies[p, dx].wait_recv()
+                take(p, h, other)
+
+    near, far = range(n_ep // 2), range(n_ep // 2, n_ep)
+    group_rows = rows // 2
+    lane = lax.broadcasted_iota(jnp.int32, (group_rows, table.shape[2]), 1)
+    first = (me_z * 2 + me_t) * local
+
+    def experts(group, low, high, load):
+        span = slice(group[0] * block, group[0] * block + group_rows)
+        blocks = slice(group[0], group[0] + len(group))
+        total = jnp.sum(
+            squares[blocks].reshape(group_rows, LANES), axis=1, keepdims=True
+        )
+        inverse = lax.rsqrt(total / width + EPSILON)
+
+        def expert(j, carry):
+            if load:
+                weight_copy(0, j).wait()
+                weight_copy(1, j).wait()
+            both = lax.dot_general(
+                xg[span], wgu[j], (((1,), (1,)), ((), ())), preferred_element_type=jnp.float32
+            )
+            weight = jnp.sum(
+                jnp.where(
+                    lane == first + j,
+                    table[blocks].reshape(group_rows, table.shape[2]),
+                    0.0,
+                ),
+                axis=1,
+                keepdims=True,
+            )
+            gate = both[:, :hidden_units] * inverse
+            silu = gate / (1.0 + jnp.exp(jnp.minimum(-gate, 88.0)))
+            act[span, pl.ds(pl.multiple_of(j * hidden_units, hidden_units), hidden_units)] = (
+                silu * (both[:, hidden_units:] * (inverse * weight))
+            ).astype(jnp.bfloat16)
+            return carry
+
+        lax.fori_loop(low, high, expert, 0)
+
+    b_copies, c_copies = {}, {}
+
+    def down(group):
+        span = slice(group[0] * block, group[0] * block + group_rows)
+        order = [*range(1, n_half), 0]
+
+        def columns_of(h, t):
+            columns = pl.ds(pl.multiple_of((h * 2 + t) * piece, piece), piece)
+            return jnp.dot(act[span], wd[:, columns], preferred_element_type=jnp.float32)
+
+        side = group[0] // len(group)
+        a_copies = {}
+        for dx in order:
+            h = lax.rem(me_h + dx, n_half)
+            a_out[dx, span] = columns_of(h, other).astype(jnp.bfloat16)
+            a_copies[dx] = go(
                 remote(
-                    here,
-                    here,
-                    hx_s.at[dx, d],
-                    hx_r.at[dx, d],
-                    half=lax.rem(me_h + dx, n_half),
+                    a_out.at[dx, span_of(span)],
+                    a_in.at[dx, span_of(span)],
+                    a_s.at[dx, side],
+                    a_r.at[dx, side],
+                    tp=other,
                 )
             )
-        t_copies[d, 0] = go(remote(here, here, ht_s.at[0, d], ht_r.at[0, d], tp=other))
-        take(z, me_h, me_t)
-    for d in range(n_ep):
-        z = lax.rem(me_z - d + n_ep, n_ep)
-        for dx in range(1, n_half):
-            h = lax.rem(me_h - dx + n_half, n_half)
-            x_copies[d, dx].wait_recv()
-            here = hid.at[z, h, me_t]
-            t_copies[d, dx] = go(remote(here, here, ht_s.at[dx, d], ht_r.at[dx, d], tp=other))
-            take(z, h, me_t)
-    for dx in range(n_half):
-        for d in range(n_ep):
-            z = lax.rem(me_z - d + n_ep, n_ep)
-            h = lax.rem(me_h - dx + n_half, n_half)
-            t_copies[d, dx].wait_recv()
-            take(z, h, other)
-    for copy in table_copies:
-        copy.wait_recv()
-
-    total = jnp.sum(squares[...].reshape(rows, LANES), axis=1, keepdims=True)
-    inverse = lax.rsqrt(total / width + EPSILON)
-    lane = lax.broadcasted_iota(jnp.int32, (rows, table.shape[2]), 1)
-    first = (me_z * 2 + me_t) * local
-
-    def expert(j, carry):
-        weight_copy(0, j).wait()
-        weight_copy(1, j).wait()
-        normed = xg[...]
-        contract = (((1,), (1,)), ((), ()))
-        gate = lax.dot_general(normed, wg[j], contract, preferred_element_type=jnp.float32)
-        up = lax.dot_general(normed, wu[j], contract, preferred_element_type=jnp.float32)
-        weight = jnp.sum(
-            jnp.where(lane == first + j, table[...].reshape(rows, table.shape[2]), 0.0),
-            axis=1,
-            keepdims=True,
-        )
-        gate = gate * inverse
-        silu = gate / (1.0 + jnp.exp(jnp.minimum(-gate, 88.0)))
-        act[:, pl.ds(pl.multiple_of(j * hidden_units, hidden_units), hidden_units)] = (
-            silu * (up * (inverse * weight))
-        ).astype(jnp.bfloat16)
-        return carry
-
-    lax.fori_loop(0, local, expert, 0)
-    for j in range(local):
-        weight_copy(2, j).wait()
-
-    def down(h, t):
-        columns = pl.ds(pl.multiple_of((h * 2 + t) * piece, piece), piece)
-        return jnp.dot(act[...], wd[:, columns], preferred_element_type=jnp.float32)
-
-    b_copies = {}
-    for dx in [*range(1, n_half), 0]:
-        h = lax.rem(me_h + dx, n_half)
-        a_out[dx] = down(h, other).astype(jnp.bfloat16)
-        a_copy = go(remote(a_out.at[dx], a_in.at[dx], a_s.at[dx], a_r.at[dx], tp=other))
-        mine[...] = down(h, me_t)
-        a_copy.wait_recv()
-        if dx > 0:
-            b_out[dx] = (mine[...] + a_in[dx].astype(jnp.float32)).astype(jnp.bfloat16)
-            for d in [*range(1, n_ep), 0]:
-                z = lax.rem(me_z + d, n_ep)
-                part = pl.ds(pl.multiple_of(z * block, block), block)
-                b_copies[dx, d] = go(
+        for dx in order:
+            h = lax.rem(me_h + dx, n_half)
+            kept[span] = columns_of(h, me_t)
+            a_copies[dx].wait_recv()
+            total = kept[span] + a_in[dx, span].astype(jnp.float32)
+            if dx == 0:
+                kept[span] = total
+                continue
+            b_out[dx, span] = total.astype(jnp.bfloat16)
+            for p in reversed(group):
+                part = pl.ds(p * block, block)
+                b_copies[p, dx] = go(
                     remote(
                         b_out.at[dx, part],
                         b_in.at[dx, part],
-                        b_s.at[dx, d],
-                        b_r.at[dx, d],
+                        b_s.at[dx, p],
+                        b_r.at[dx, p],
                         half=h,
                     )
                 )
-        else:
-            kept[...] = mine[...] + a_in[dx].astype(jnp.float32)
-    c_copies = {}
-    for d in [*range(1, n_ep), 0]:
-        z = lax.rem(me_z + d, n_ep)
-        part = pl.ds(pl.multiple_of(z * block, block), block)
-        total = kept[part]
-        for dx in range(1, n_half):
-            b_copies[dx, d].wait_recv()
-            total = total + b_in[dx, part].astype(jnp.float32)
-        if d > 0:
-            c_out[d] = total.astype(jnp.bfloat16)
-            c_copies[d] = go(remote(c_out.at[d], c_in.at[d], c_s.at[d], c_r.at[d], ep=z))
-        else:
-            own_hidden[...] += total
+
+    def send_back(group):
+        for p in reversed(group):
+            part = slice(p * block, (p + 1) * block)
+            total = kept[part]
+            for dx in range(1, n_half):
+                b_copies[p, dx].wait_recv()
+                total = total + b_in[dx, part].astype(jnp.float32)
+            if p > 0:
+                c_out[p] = total.astype(jnp.bfloat16)
+                c_copies[p] = go(
+                    remote(c_out.at[p], c_in.at[p], c_s.at[p], c_r.at[p], ep=partner(me_z, p))
+                )
+            else:
+                own_hidden[...] += total
+
+    spread_own(near)
+    for copy in gain_copies:
+        copy.wait_recv()
+    squares[...] = jnp.zeros_like(squares)
+    spread_crossed(near)
+    for copy in table_copies:
+        copy.wait_recv()
+    take_all(near)
+    cuts = [0, local // 4, local * 5 // 8, local]
+    experts(near, cuts[0], cuts[1], True)
+    spread_own(far)
+    experts(near, cuts[1], cuts[2], True)
+    spread_crossed(far)
+    experts(near, cuts[2], cuts[3], True)
+    for j in range(local):
+        weight_copy(2, j).wait()
+    down(near)
+    take_all(far)
+    experts(far, 0, local, False)
+    send_back(near)
+    down(far)
+    send_back(far)
     result = own_hidden[...]
-    for d in range(1, n_ep):
-        c_copies[d].wait_recv()
-        result = result + c_in[d].astype(jnp.float32)
+    for p in range(1, n_ep):
+        c_copies[p].wait_recv()
+        result = result + c_in[p].astype(jnp.float32)
     out_ref[...] = result.astype(jnp.bfloat16)
     for copy in sent:
         copy.wait_send()
@@ -551,8 +608,7 @@
         ((requests, context, head_size), bf16),
         ((requests, context, head_size), bf16),
         (out_weight.shape, bf16),
-        (w_gate.shape, bf16),
-        (w_up.shape, bf16),
+        ((local, 2 * hidden_units, width), bf16),
         ((local * hidden_units, width), bf16),
         (queries.shape, f32),
         ((n_half,) + queries.shape, bf16),
@@ -567,7 +623,6 @@
         ((rows, local * hidden_units), bf16),
         ((n_half, rows, piece), bf16),
         ((n_half, rows, piece), bf16),
-        ((rows, piece), f32),
         ((n_half, rows, piece), bf16),
         ((n_half, rows, piece), bf16),
         ((rows, piece), f32),
@@ -578,6 +633,8 @@
     fits = (
         held * 5 // 4 < VMEM_BYTES
         and n_tp == 2
+        and n_ep > 1
+        and n_ep & (n_ep - 1) == 0
         and key_heads == 1
         and hidden_units % LANES == 0
         and piece % LANES == 0
@@ -604,8 +661,8 @@
         dma((n_half, n_ep)),
         dma((n_half, n_ep)),
         dma((n_half, n_ep)),
-        dma((n_half,)),
-        dma((n_half,)),
+        dma((n_half, 2)),
+        dma((n_half, 2)),
         dma((n_half, n_ep)),
         dma((n_half, n_ep)),
         dma((n_ep,)),
@@ -626,11 +683,11 @@
         queries,
         new_keys,
         new_values,
-        lengths.reshape(requests, 1),
+        lengths.reshape(1, requests),
         residual,
         norm_gain.reshape(1, half_width),
-        expert_ids,
-        gate_weights,
+        expert_ids.T,
+        gate_weights.T,
         cache_keys.reshape(requests, context, head_size),
         cache_values.reshape(requests, context, head_size),
         out_weight,

time: 64.5 us -> 68.8 us (1.067)
  Pallas kernels: 58.7 us -> 67.2 us
  local copies, waits for them, and re-layouts: 5.56 us -> 1.47 us
    pallas_call x1, Pallas kernels: 58.7 us -> 67.2 us  [on_device(): pl.pallas_call(functools.partial(layer_kernel, dict(ep=n_ep, half=n_half)...]
    unnamed x3 -> x1, local copies, waits for them, and re-layouts: 4.22 us -> 1.47 us
    reshape x1 -> x0, local copies, waits for them, and re-layouts: 1.33 us -> none  [on_device(): lengths.reshape(requests, 1)]
where the time goes in v2:
time: 68.8 us; the launch traced here: 68.6 us
  Pallas kernels  67.2 us (98%)
  local copies, waits for them, and re-layouts  1.47 us (2%)
    pallas_call x1, Pallas kernels, on_device(): pl.pallas_call(functools.partial(layer_kernel, dict(ep=n_ep, half=n_half)...  67.2 us
    unnamed x1, local copies, waits for them, and re-layouts  1.47 us

profile of v2, /device:TPU:0, one launch (start us, length us, event | category | flops | bytes accessed | tf_op | source)
XLA Modules:
  0.0 68.6 jit_solution(3238561695421535078)
XLA Ops:
  0.0 67.2 %shard_map.136 = bf16[64,512]{1,0:T(8,128)(2,1)} custom-call(bf16[32,1024]{1,0:T(8,128)(2,1)} %q_ref.1, bf16[32,128]{1,0:T(8,128)(2,1)} %nk_ref.1, bf16[32,128]{1,0:T(8,128)(2,1)} %nv_ref.1, s32[1,32]{1,0:T(1,128)} %bitcast.13, bf16[64,1024]{1,0:T(8,128)(2,1)} %res_ref.1, f32[1,1024]{1,0:T(1,128)} %bitcast.10, s32[8,64]{1,0:T(8,128)} %bitcast.11, ...), custom_call_target="tpu_custom_call" | custom-call | tf_op jit(solution)/shard_map/pallas_call | solution.py:673
  67.2 1.5 %copy.16 = bf16[64,512]{1,0:T(8,128)(2,1)} copy(bf16[64,512]{1,0:T(8,128)(2,1)} %shard_map.136) | data formatting | bytes 131072

commit v3 on v2

--- a/solution.py
+++ b/solution.py
@@ -167,10 +167,6 @@
             index = index + bit - 2 * bit * (index // bit % 2)
         bit *= 2
     return index
-
-
-def span_of(span):
-    return pl.ds(span.start, span.stop - span.start)
 
 
 def layer_kernel(
@@ -203,14 +199,15 @@
     mix_in,
     own_hidden,
     hid,
-    xg,
+    xt,
     squares,
+    sums,
     act,
     a_out,
     a_in,
     b_out,
     b_in,
-    kept,
+    mine,
     c_out,
     c_in,
     load_sem,
@@ -330,11 +327,11 @@
             att_f[part, h * head_size : (h + 1) * head_size] = mixture[h * step : (h + 1) * step]
     att[me_h] = att_f[...].astype(jnp.bfloat16)
     gates = gw_ref[...] / jnp.sum(gw_ref[...], axis=0, keepdims=True)
-    expert_row = lax.broadcasted_iota(jnp.int32, (table.shape[2], block), 0)
-    own_table = jnp.zeros((table.shape[2], block), jnp.float32)
+    expert_row = lax.broadcasted_iota(jnp.int32, (table.shape[1], block), 0)
+    own_table = jnp.zeros((table.shape[1], block), jnp.float32)
     for k in range(ids_ref.shape[0]):
         own_table += jnp.where(expert_row == ids_ref[k : k + 1, :], gates[k : k + 1, :], 0.0)
-    table[0] = own_table.T
+    table[0] = own_table
     gain[me_h] = jnp.broadcast_to(gain_ref[...], gain.shape[1:])
 
     pl.semaphore_wait(barrier, 1 + (n_half - 1) + (n_ep - 1))
@@ -402,18 +399,19 @@
     }
     x_copies, t_copies = {}, {}
 
-    def take(p, h, t):
-        value = hid[p, h, t].astype(jnp.float32)
-        square = value * value
-        total = square[:, :LANES]
-        for k in range(1, piece // LANES):
-            total = total + square[:, k * LANES : (k + 1) * LANES]
-        squares[p] += total
+    def take(h, t):
+        gain_columns = pl.ds(pl.multiple_of(t * piece, piece), piece)
+        scaled = []
+        for p in range(n_ep):
+            value = hid[p, h, t].astype(jnp.float32)
+            square = value * value
+            total = square[:, :LANES]
+            for k in range(1, piece // LANES):
+                total = total + square[:, k * LANES : (k + 1) * LANES]
+            squares[p] += total
+            scaled.append(value * gain[h, 0:1, gain_columns])
         columns = pl.ds(pl.multiple_of((h * 2 + t) * piece, piece), piece)
-        gain_columns = pl.ds(pl.multiple_of(t * piece, piece), piece)
-        xg[p * block : (p + 1) * block, columns] = (value * gain[h, 0:1, gain_columns]).astype(
-            jnp.bfloat16
-        )
+        xt[columns, :] = jnp.concatenate(scaled, axis=0).T.astype(jnp.bfloat16)
 
     def to_sibling(p, dx, h):
         here = hid.at[p, h, me_t]
@@ -442,134 +440,103 @@
                 x_copies[p, dx].wait_recv()
                 to_sibling(p, dx, lax.rem(me_h - dx + n_half, n_half))
 
-    def take_all(group):
-        for dx in range(n_half):
-            for p in group:
-                h = lax.rem(me_h - dx + n_half, n_half)
-                take(p, h, me_t)
-                t_copies[p, dx].wait_recv()
-                take(p, h, other)
-
-    near, far = range(n_ep // 2), range(n_ep // 2, n_ep)
-    group_rows = rows // 2
-    lane = lax.broadcasted_iota(jnp.int32, (group_rows, table.shape[2]), 1)
-    first = (me_z * 2 + me_t) * local
-
-    def experts(group, low, high, load):
-        span = slice(group[0] * block, group[0] * block + group_rows)
-        blocks = slice(group[0], group[0] + len(group))
-        total = jnp.sum(
-            squares[blocks].reshape(group_rows, LANES), axis=1, keepdims=True
-        )
-        inverse = lax.rsqrt(total / width + EPSILON)
-
-        def expert(j, carry):
-            if load:
-                weight_copy(0, j).wait()
-                weight_copy(1, j).wait()
-            both = lax.dot_general(
-                xg[span], wgu[j], (((1,), (1,)), ((), ())), preferred_element_type=jnp.float32
-            )
-            weight = jnp.sum(
-                jnp.where(
-                    lane == first + j,
-                    table[blocks].reshape(group_rows, table.shape[2]),
-                    0.0,
-                ),
-                axis=1,
-                keepdims=True,
-            )
-            gate = both[:, :hidden_units] * inverse
-            silu = gate / (1.0 + jnp.exp(jnp.minimum(-gate, 88.0)))
-            act[span, pl.ds(pl.multiple_of(j * hidden_units, hidden_units), hidden_units)] = (
-                silu * (both[:, hidden_units:] * (inverse * weight))
-            ).astype(jnp.bfloat16)
-            return carry
-
-        lax.fori_loop(low, high, expert, 0)
-
-    b_copies, c_copies = {}, {}
-
-    def down(group):
-        span = slice(group[0] * block, group[0] * block + group_rows)
-        order = [*range(1, n_half), 0]
-
-        def columns_of(h, t):
-            columns = pl.ds(pl.multiple_of((h * 2 + t) * piece, piece), piece)
-            return jnp.dot(act[span], wd[:, columns], preferred_element_type=jnp.float32)
-
-        side = group[0] // len(group)
-        a_copies = {}
-        for dx in order:
-            h = lax.rem(me_h + dx, n_half)
-            a_out[dx, span] = columns_of(h, other).astype(jnp.bfloat16)
-            a_copies[dx] = go(
+    def product(dx, j):
+        h = lax.rem(me_h - dx + n_half, n_half)
+        span = pl.ds(pl.multiple_of(h * 2 * piece, 2 * piece), 2 * piece)
+        return jnp.dot(wgu[j, :, span], xt[span, :], preferred_element_type=jnp.float32)
+
+    def finish(j, inverse):
+        weight = jnp.concatenate(
+            [table[p, pl.ds((me_z * 2 + me_t) * local + j, 1), :] for p in range(n_ep)], axis=1
+        )
+        gate = sums[j, :hidden_units] * inverse
+        silu = gate / (1.0 + jnp.exp(jnp.minimum(-gate, 88.0)))
+        value = silu * (sums[j, hidden_units:] * (inverse * weight))
+        act[:, j * hidden_units : (j + 1) * hidden_units] = value.T.astype(jnp.bfloat16)
+
+    a_copies, b_copies, c_copies = {}, {}, {}
+
+    def down(h, t):
+        columns = pl.ds(pl.multiple_of((h * 2 + t) * piece, piece), piece)
+        return jnp.dot(act[...], wd[:, columns], preferred_element_type=jnp.float32)
+
+    def send_across(dx):
+        a_out[dx] = down(lax.rem(me_h + dx, n_half), other).astype(jnp.bfloat16)
+        a_copies[dx] = go(remote(a_out.at[dx], a_in.at[dx], a_s.at[dx], a_r.at[dx], tp=other))
+
+    def send_over(dx):
+        a_copies[dx].wait_recv()
+        total = mine[dx] + a_in[dx].astype(jnp.float32)
+        if dx == 0:
+            mine[dx] = total
+            return
+        b_out[dx] = total.astype(jnp.bfloat16)
+        for p in reversed(range(n_ep)):
+            part = pl.ds(p * block, block)
+            b_copies[p, dx] = go(
                 remote(
-                    a_out.at[dx, span_of(span)],
-                    a_in.at[dx, span_of(span)],
-                    a_s.at[dx, side],
-                    a_r.at[dx, side],
-                    tp=other,
+                    b_out.at[dx, part],
+                    b_in.at[dx, part],
+                    b_s.at[dx, p],
+                    b_r.at[dx, p],
+                    half=lax.rem(me_h + dx, n_half),
                 )
             )
-        for dx in order:
-            h = lax.rem(me_h + dx, n_half)
-            kept[span] = columns_of(h, me_t)
-            a_copies[dx].wait_recv()
-            total = kept[span] + a_in[dx, span].astype(jnp.float32)
-            if dx == 0:
-                kept[span] = total
-                continue
-            b_out[dx, span] = total.astype(jnp.bfloat16)
-            for p in reversed(group):
-                part = pl.ds(p * block, block)
-                b_copies[p, dx] = go(
-                    remote(
-                        b_out.at[dx, part],
-                        b_in.at[dx, part],
-                        b_s.at[dx, p],
-                        b_r.at[dx, p],
-                        half=h,
-                    )
-                )
-
-    def send_back(group):
-        for p in reversed(group):
-            part = slice(p * block, (p + 1) * block)
-            total = kept[part]
-            for dx in range(1, n_half):
-                b_copies[p, dx].wait_recv()
-                total = total + b_in[dx, part].astype(jnp.float32)
-            if p > 0:
-                c_out[p] = total.astype(jnp.bfloat16)
-                c_copies[p] = go(
-                    remote(c_out.at[p], c_in.at[p], c_s.at[p], c_r.at[p], ep=partner(me_z, p))
-                )
-            else:
-                own_hidden[...] += total
-
-    spread_own(near)
+
+    spread_own(range(n_ep))
     for copy in gain_copies:
         copy.wait_recv()
     squares[...] = jnp.zeros_like(squares)
-    spread_crossed(near)
+    take(me_h, me_t)
+    for p in range(n_ep):
+        t_copies[p, 0].wait_recv()
+    take(me_h, other)
+    for j in range(local):
+        weight_copy(0, j).wait()
+        weight_copy(1, j).wait()
+        sums[j] = product(0, j)
+        if j == local * 3 // 8:
+            spread_crossed(range(n_ep // 2))
+        if j == local * 3 // 4:
+            spread_crossed(range(n_ep // 2, n_ep))
+    for dx in range(1, n_half):
+        h = lax.rem(me_h - dx + n_half, n_half)
+        take(h, me_t)
+        for p in range(n_ep):
+            t_copies[p, dx].wait_recv()
+        take(h, other)
     for copy in table_copies:
         copy.wait_recv()
-    take_all(near)
-    cuts = [0, local // 4, local * 5 // 8, local]
-    experts(near, cuts[0], cuts[1], True)
-    spread_own(far)
-    experts(near, cuts[1], cuts[2], True)
-    spread_crossed(far)
-    experts(near, cuts[2], cuts[3], True)
+    total = jnp.sum(squares[...].reshape(rows, LANES).T, axis=0, keepdims=True)
+    inverse = lax.rsqrt(total / width + EPSILON)
+    for j in range(local):
+        for dx in range(1, n_half):
+            sums[j] += product(dx, j)
+        if j > 0:
+            finish(j - 1, inverse)
+    finish(local - 1, inverse)
     for j in range(local):
         weight_copy(2, j).wait()
-    down(near)
-    take_all(far)
-    experts(far, 0, local, False)
-    send_back(near)
-    down(far)
-    send_back(far)
+    order = [*range(1, n_half), 0]
+    for k, dx in enumerate(order):
+        send_across(dx)
+        if k > 0:
+            send_over(order[k - 1])
+        mine[dx] = down(lax.rem(me_h + dx, n_half), me_t)
+    send_over(0)
+    for p in reversed(range(n_ep)):
+        part = slice(p * block, (p + 1) * block)
+        total = mine[0, part]
+        for dx in range(1, n_half):
+            b_copies[p, dx].wait_recv()
+            total = total + b_in[dx, part].astype(jnp.float32)
+        if p > 0:
+            c_out[p] = total.astype(jnp.bfloat16)
+            c_copies[p] = go(
+                remote(c_out.at[p], c_in.at[p], c_s.at[p], c_r.at[p], ep=partner(me_z, p))
+            )
+        else:
+            own_hidden[...] += total
     result = own_hidden[...]
     for p in range(1, n_ep):
         c_copies[p].wait_recv()
@@ -602,7 +569,7 @@
     local, hidden_units, width = w_gate.shape
     piece = half_width // 2
     rows = n_ep * block
-    lanes = -(-(local * n_ep * n_tp) // LANES) * LANES
+    experts = local * n_ep * n_tp
     bf16, f32 = jnp.bfloat16, jnp.float32
     buffers = [
         ((requests, context, head_size), bf16),
@@ -613,25 +580,26 @@
         (queries.shape, f32),
         ((n_half,) + queries.shape, bf16),
         ((n_half, ROW_TILE, half_width), f32),
-        ((n_ep, block, lanes), f32),
+        ((n_ep, experts, block), f32),
         ((block, piece), bf16),
         ((block, piece), bf16),
         ((block, piece), f32),
         ((n_ep, n_half, n_tp, block, piece), bf16),
-        ((rows, width), bf16),
+        ((width, rows), bf16),
         ((n_ep, block, LANES), f32),
+        ((local, 2 * hidden_units, rows), f32),
         ((rows, local * hidden_units), bf16),
         ((n_half, rows, piece), bf16),
         ((n_half, rows, piece), bf16),
         ((n_half, rows, piece), bf16),
         ((n_half, rows, piece), bf16),
-        ((rows, piece), f32),
+        ((n_half, rows, piece), f32),
         ((n_ep, block, piece), bf16),
         ((n_ep, block, piece), bf16),
     ]
     held = sum(math.prod(shape) * jnp.dtype(kind).itemsize for shape, kind in buffers)
     fits = (
-        held * 5 // 4 < VMEM_BYTES
+        held * 9 // 8 < VMEM_BYTES
         and n_tp == 2
         and n_ep > 1
         and n_ep & (n_ep - 1) == 0
@@ -661,8 +629,8 @@
         dma((n_half, n_ep)),
         dma((n_half, n_ep)),
         dma((n_half, n_ep)),
-        dma((n_half, 2)),
-        dma((n_half, 2)),
+        dma((n_half,)),
+        dma((n_half,)),
         dma((n_half, n_ep)),
         dma((n_half, n_ep)),
         dma((n_ep,)),

time: 68.8 us -> 58.8 us (0.85)
  Pallas kernels: 67.2 us -> 57.2 us
    pallas_call x1, Pallas kernels: 67.2 us -> 57.2 us  [on_device(): pl.pallas_call(functools.partial(layer_kernel, dict(ep=n_ep, half=n_half)...]
where the time goes in v3:
time: 58.8 us; the launch traced here: 58.7 us
  Pallas kernels  57.2 us (97%)
  local copies, waits for them, and re-layouts  1.47 us (2%)
    pallas_call x1, Pallas kernels, on_device(): pl.pallas_call(functools.partial(layer_kernel, dict(ep=n_ep, half=n_half)...  57.2 us
    unnamed x1, local copies, waits for them, and re-layouts  1.47 us

profile of v3, /device:TPU:0, one launch (start us, length us, event | category | flops | bytes accessed | tf_op | source)
XLA Modules:
  0.0 58.7 jit_solution(16963907085671388375)
XLA Ops:
  0.0 57.2 %shard_map.136 = bf16[64,512]{1,0:T(8,128)(2,1)} custom-call(bf16[32,1024]{1,0:T(8,128)(2,1)} %q_ref.1, bf16[32,128]{1,0:T(8,128)(2,1)} %nk_ref.1, bf16[32,128]{1,0:T(8,128)(2,1)} %nv_ref.1, s32[1,32]{1,0:T(1,128)} %bitcast.13, bf16[64,1024]{1,0:T(8,128)(2,1)} %res_ref.1, f32[1,1024]{1,0:T(1,128)} %bitcast.10, s32[8,64]{1,0:T(8,128)} %bitcast.11, ...), custom_call_target="tpu_custom_call" | custom-call | tf_op jit(solution)/shard_map/pallas_call | solution.py:641
  57.2 1.5 %copy.16 = bf16[64,512]{1,0:T(8,128)(2,1)} copy(bf16[64,512]{1,0:T(8,128)(2,1)} %shard_map.136) | data formatting | bytes 131072

commit v4 on v3

--- a/solution.py
+++ b/solution.py
@@ -167,6 +167,20 @@
             index = index + bit - 2 * bit * (index // bit % 2)
         bit *= 2
     return index
+
+
+def each(low, high, body):
+    many = 4
+    whole = (high - low) // many
+
+    def several(i, carry):
+        for k in range(many):
+            body(low + i * many + k)
+        return carry
+
+    lax.fori_loop(0, whole, several, 0)
+    for k in range(low + whole * many, high):
+        body(k)
 
 
 def layer_kernel(
@@ -261,11 +275,12 @@
         part = pl.ds(j * hidden_units, hidden_units)
         return pltpu.make_async_copy(wd_hbm.at[part], wd.at[part], w_sem.at[k, j])
 
-    for j in range(local):
-        weight_copy(0, j).start()
-        weight_copy(1, j).start()
-    for j in range(local):
-        weight_copy(2, j).start()
+    def start_weights(kinds, low, high):
+        for j in range(low, high):
+            for k in kinds:
+                weight_copy(k, j).start()
+
+    start_weights((0, 1), 0, local // 2)
 
     barrier = pltpu.get_barrier_semaphore()
     pl.semaphore_signal(barrier, inc=1, device_id={"tp": other}, device_id_type=MESH)
@@ -347,6 +362,7 @@
         )
         for d in range(1, n_half)
     ]
+    start_weights((0, 1), local // 2, local)
     gain_copies = [
         go(
             remote(
@@ -397,12 +413,15 @@
         )
         for p in range(1, n_ep)
     }
+    start_weights((2,), 0, local)
     x_copies, t_copies = {}, {}
 
-    def take(h, t):
+    near, far = range(n_ep // 2), range(n_ep // 2, n_ep)
+
+    def take(group, h, t):
         gain_columns = pl.ds(pl.multiple_of(t * piece, piece), piece)
         scaled = []
-        for p in range(n_ep):
+        for p in group:
             value = hid[p, h, t].astype(jnp.float32)
             square = value * value
             total = square[:, :LANES]
@@ -411,7 +430,9 @@
             squares[p] += total
             scaled.append(value * gain[h, 0:1, gain_columns])
         columns = pl.ds(pl.multiple_of((h * 2 + t) * piece, piece), piece)
-        xt[columns, :] = jnp.concatenate(scaled, axis=0).T.astype(jnp.bfloat16)
+        xt[columns, group[0] * block : (group[-1] + 1) * block] = (
+            jnp.concatenate(scaled, axis=0).T.astype(jnp.bfloat16)
+        )
 
     def to_sibling(p, dx, h):
         here = hid.at[p, h, me_t]
@@ -440,19 +461,19 @@
                 x_copies[p, dx].wait_recv()
                 to_sibling(p, dx, lax.rem(me_h - dx + n_half, n_half))
 
-    def product(dx, j):
-        h = lax.rem(me_h - dx + n_half, n_half)
-        span = pl.ds(pl.multiple_of(h * 2 * piece, 2 * piece), 2 * piece)
+    def product(h, t, j):
+        span = pl.ds(pl.multiple_of((h * 2 + t) * piece, piece), piece)
         return jnp.dot(wgu[j, :, span], xt[span, :], preferred_element_type=jnp.float32)
 
-    def finish(j, inverse):
+    def finish(h, inverse, j):
         weight = jnp.concatenate(
             [table[p, pl.ds((me_z * 2 + me_t) * local + j, 1), :] for p in range(n_ep)], axis=1
         )
-        gate = sums[j, :hidden_units] * inverse
+        both = sums[j] + product(h, other, j)
+        gate = both[:hidden_units] * inverse
         silu = gate / (1.0 + jnp.exp(jnp.minimum(-gate, 88.0)))
-        value = silu * (sums[j, hidden_units:] * (inverse * weight))
-        act[:, j * hidden_units : (j + 1) * hidden_units] = value.T.astype(jnp.bfloat16)
+        value = silu * (both[hidden_units:] * (inverse * weight))
+        act[:, pl.ds(pl.multiple_of(j * hidden_units, hidden_units), hidden_units)] = value.T.astype(jnp.bfloat16)
 
     a_copies, b_copies, c_copies = {}, {}, {}
 
@@ -470,77 +491,86 @@
         if dx == 0:
             mine[dx] = total
             return
-        b_out[dx] = total.astype(jnp.bfloat16)
+        b_out[dx - 1] = total.astype(jnp.bfloat16)
         for p in reversed(range(n_ep)):
             part = pl.ds(p * block, block)
             b_copies[p, dx] = go(
                 remote(
-                    b_out.at[dx, part],
-                    b_in.at[dx, part],
+                    b_out.at[dx - 1, part],
+                    b_in.at[dx - 1, part],
                     b_s.at[dx, p],
                     b_r.at[dx, p],
                     half=lax.rem(me_h + dx, n_half),
                 )
             )
 
-    spread_own(range(n_ep))
+    spread_own(near)
     for copy in gain_copies:
         copy.wait_recv()
     squares[...] = jnp.zeros_like(squares)
-    take(me_h, me_t)
-    for p in range(n_ep):
-        t_copies[p, 0].wait_recv()
-    take(me_h, other)
-    for j in range(local):
+    take(near, me_h, me_t)
+    spread_own(far)
+    take(far, me_h, me_t)
+    def first_piece(j):
         weight_copy(0, j).wait()
         weight_copy(1, j).wait()
-        sums[j] = product(0, j)
-        if j == local * 3 // 8:
-            spread_crossed(range(n_ep // 2))
-        if j == local * 3 // 4:
-            spread_crossed(range(n_ep // 2, n_ep))
+        sums[j] = product(me_h, me_t, j)
+
+    def next_piece(h, t, j):
+        sums[j] += product(h, t, j)
+
+    each(0, local * 3 // 4, first_piece)
+    spread_crossed(near)
+    each(local * 3 // 4, local, first_piece)
+    for group in (near, far):
+        for p in group:
+            t_copies[p, 0].wait_recv()
+        take(group, me_h, other)
+    each(0, local // 2, functools.partial(next_piece, me_h, other))
+    spread_crossed(far)
+    each(local // 2, local, functools.partial(next_piece, me_h, other))
+    for copy in table_copies:
+        copy.wait_recv()
     for dx in range(1, n_half):
         h = lax.rem(me_h - dx + n_half, n_half)
-        take(h, me_t)
-        for p in range(n_ep):
-            t_copies[p, dx].wait_recv()
-        take(h, other)
-    for copy in table_copies:
-        copy.wait_recv()
-    total = jnp.sum(squares[...].reshape(rows, LANES).T, axis=0, keepdims=True)
-    inverse = lax.rsqrt(total / width + EPSILON)
-    for j in range(local):
-        for dx in range(1, n_half):
-            sums[j] += product(dx, j)
-        if j > 0:
-            finish(j - 1, inverse)
-    finish(local - 1, inverse)
+        take(near, h, me_t)
+        take(far, h, me_t)
+        each(0, local, functools.partial(next_piece, h, me_t))
+        for group in (near, far):
+            for p in group:
+                t_copies[p, dx].wait_recv()
+            take(group, h, other)
+        if dx == n_half - 1:
+            total = jnp.sum(squares[...].reshape(rows, LANES).T, axis=0, keepdims=True)
+            inverse = lax.rsqrt(total / width + EPSILON)
+        if dx < n_half - 1:
+            each(0, local, functools.partial(next_piece, h, other))
+        else:
+            each(0, local, functools.partial(finish, h, inverse))
     for j in range(local):
         weight_copy(2, j).wait()
     order = [*range(1, n_half), 0]
-    for k, dx in enumerate(order):
+    for dx in order:
         send_across(dx)
-        if k > 0:
-            send_over(order[k - 1])
         mine[dx] = down(lax.rem(me_h + dx, n_half), me_t)
-    send_over(0)
+        send_over(dx)
     for p in reversed(range(n_ep)):
         part = slice(p * block, (p + 1) * block)
         total = mine[0, part]
         for dx in range(1, n_half):
             b_copies[p, dx].wait_recv()
-            total = total + b_in[dx, part].astype(jnp.float32)
+            total = total + b_in[dx - 1, part].astype(jnp.float32)
         if p > 0:
-            c_out[p] = total.astype(jnp.bfloat16)
+            c_out[p - 1] = total.astype(jnp.bfloat16)
             c_copies[p] = go(
-                remote(c_out.at[p], c_in.at[p], c_s.at[p], c_r.at[p], ep=partner(me_z, p))
+                remote(c_out.at[p - 1], c_in.at[p - 1], c_s.at[p], c_r.at[p], ep=partner(me_z, p))
             )
         else:
             own_hidden[...] += total
     result = own_hidden[...]
     for p in range(1, n_ep):
         c_copies[p].wait_recv()
-        result = result + c_in[p].astype(jnp.float32)
+        result = result + c_in[p - 1].astype(jnp.float32)
     out_ref[...] = result.astype(jnp.bfloat16)
     for copy in sent:
         copy.wait_send()
@@ -591,21 +621,23 @@
         ((rows, local * hidden_units), bf16),
         ((n_half, rows, piece), bf16),
         ((n_half, rows, piece), bf16),
-        ((n_half, rows, piece), bf16),
-        ((n_half, rows, piece), bf16),
+        ((n_half - 1, rows, piece), bf16),
+        ((n_half - 1, rows, piece), bf16),
         ((n_half, rows, piece), f32),
-        ((n_ep, block, piece), bf16),
-        ((n_ep, block, piece), bf16),
+        ((n_ep - 1, block, piece), bf16),
+        ((n_ep - 1, block, piece), bf16),
     ]
     held = sum(math.prod(shape) * jnp.dtype(kind).itemsize for shape, kind in buffers)
     fits = (
-        held * 9 // 8 < VMEM_BYTES
+        held * 17 // 16 < VMEM_BYTES
         and n_tp == 2
         and n_ep > 1
         and n_ep & (n_ep - 1) == 0
         and key_heads == 1
         and hidden_units % LANES == 0
         and piece % LANES == 0
+        and n_half > 1
+        and rows % (2 * LANES) == 0
         and requests % (2 * ROW_TILE) == 0
         and block == n_half * requests
     )

time: 58.8 us -> 50.1 us (0.85)
  Pallas kernels: 57.2 us -> 48.5 us
    pallas_call x1, Pallas kernels: 57.2 us -> 48.5 us  [on_device(): pl.pallas_call(functools.partial(layer_kernel, dict(ep=n_ep, half=n_half)...]
where the time goes in v4:
time: 50.1 us; the launch traced here: 49.9 us
  Pallas kernels  48.5 us (97%)
  local copies, waits for them, and re-layouts  1.47 us (3%)
    pallas_call x1, Pallas kernels, on_device(): pl.pallas_call(functools.partial(layer_kernel, dict(ep=n_ep, half=n_half)...  48.5 us
    unnamed x1, local copies, waits for them, and re-layouts  1.47 us

profile of v4, /device:TPU:0, one launch (start us, length us, event | category | flops | bytes accessed | tf_op | source)
XLA Modules:
  0.0 49.9 jit_solution(5285160647535546683)
XLA Ops:
  0.0 48.5 %shard_map.136 = bf16[64,512]{1,0:T(8,128)(2,1)} custom-call(bf16[32,1024]{1,0:T(8,128)(2,1)} %q_ref.1, bf16[32,128]{1,0:T(8,128)(2,1)} %nk_ref.1, bf16[32,128]{1,0:T(8,128)(2,1)} %nv_ref.1, s32[1,32]{1,0:T(1,128)} %bitcast.13, bf16[64,1024]{1,0:T(8,128)(2,1)} %res_ref.1, f32[1,1024]{1,0:T(1,128)} %bitcast.10, s32[8,64]{1,0:T(8,128)} %bitcast.11, ...), custom_call_target="tpu_custom_call" | custom-call | tf_op jit(solution)/shard_map/pallas_call | solution.py:673
  48.5 1.5 %copy.16 = bf16[64,512]{1,0:T(8,128)(2,1)} copy(bf16[64,512]{1,0:T(8,128)(2,1)} %shard_map.136) | data formatting | bytes 131072

commit v5 on v4

--- a/solution.py
+++ b/solution.py
@@ -362,7 +362,7 @@
         )
         for d in range(1, n_half)
     ]
-    start_weights((0, 1), local // 2, local)
+    start_weights((0, 1), local // 2, local * 3 // 4)
     gain_copies = [
         go(
             remote(
@@ -394,6 +394,7 @@
         attended, ow[:, other_columns], preferred_element_type=jnp.float32
     ).astype(jnp.bfloat16)
     mix_copy = go(remote(mix_out, mix_in, mix_s, mix_r, tp=other))
+    start_weights((0, 1), local * 3 // 4, local)
     mixed = jnp.dot(attended, ow[:, my_columns], preferred_element_type=jnp.float32)
     mixed = mixed + res_ref[:, my_columns].astype(jnp.float32)
     mix_copy.wait_recv()
@@ -413,7 +414,6 @@
         )
         for p in range(1, n_ep)
     }
-    start_weights((2,), 0, local)
     x_copies, t_copies = {}, {}
 
     near, far = range(n_ep // 2), range(n_ep // 2, n_ep)
@@ -491,9 +491,9 @@
         if dx == 0:
             mine[dx] = total
             return
-        b_out[dx - 1] = total.astype(jnp.bfloat16)
         for p in reversed(range(n_ep)):
             part = pl.ds(p * block, block)
+            b_out[dx - 1, part] = total[p * block : (p + 1) * block].astype(jnp.bfloat16)
             b_copies[p, dx] = go(
                 remote(
                     b_out.at[dx - 1, part],
@@ -514,14 +514,15 @@
     def first_piece(j):
         weight_copy(0, j).wait()
         weight_copy(1, j).wait()
+        weight_copy(2, j).start()
         sums[j] = product(me_h, me_t, j)
 
     def next_piece(h, t, j):
         sums[j] += product(h, t, j)
 
-    each(0, local * 3 // 4, first_piece)
+    each(0, local // 2, first_piece)
     spread_crossed(near)
-    each(local * 3 // 4, local, first_piece)
+    each(local // 2, local, first_piece)
     for group in (near, far):
         for p in group:
             t_copies[p, 0].wait_recv()

time: 50.1 us -> 50.3 us (level)
  no operation moved by 1% of the time
where the time goes in v5:
time: 50.3 us; the launch traced here: 50.1 us
  Pallas kernels  48.6 us (97%)
  local copies, waits for them, and re-layouts  1.47 us (3%)
    pallas_call x1, Pallas kernels, on_device(): pl.pallas_call(functools.partial(layer_kernel, dict(ep=n_ep, half=n_half)...  48.6 us
    unnamed x1, local copies, waits for them, and re-layouts  1.47 us

profile of v5, /device:TPU:0, one launch (start us, length us, event | category | flops | bytes accessed | tf_op | source)
XLA Modules:
  0.0 50.1 jit_solution(15145372398264488469)
XLA Ops:
  0.0 48.6 %shard_map.136 = bf16[64,512]{1,0:T(8,128)(2,1)} custom-call(bf16[32,1024]{1,0:T(8,128)(2,1)} %q_ref.1, bf16[32,128]{1,0:T(8,128)(2,1)} %nk_ref.1, bf16[32,128]{1,0:T(8,128)(2,1)} %nv_ref.1, s32[1,32]{1,0:T(1,128)} %bitcast.13, bf16[64,1024]{1,0:T(8,128)(2,1)} %res_ref.1, f32[1,1024]{1,0:T(1,128)} %bitcast.10, s32[8,64]{1,0:T(8,128)} %bitcast.11, ...), custom_call_target="tpu_custom_call" | custom-call | tf_op jit(solution)/shard_map/pallas_call | solution.py:674
  48.6 1.5 %copy.16 = bf16[64,512]{1,0:T(8,128)(2,1)} copy(bf16[64,512]{1,0:T(8,128)(2,1)} %shard_map.136) | data formatting | bytes 131072

commit v6 on v5

--- a/solution.py
+++ b/solution.py
@@ -170,7 +170,7 @@
 
 
 def each(low, high, body):
-    many = 4
+    many = 2
     whole = (high - low) // many
 
     def several(i, carry):
@@ -477,12 +477,22 @@
 
     a_copies, b_copies, c_copies = {}, {}, {}
 
-    def down(h, t):
-        columns = pl.ds(pl.multiple_of((h * 2 + t) * piece, piece), piece)
-        return jnp.dot(act[...], wd[:, columns], preferred_element_type=jnp.float32)
+    def down(h, t, store):
+        tile = piece // 2
+
+        def one(k, carry):
+            columns = pl.ds(pl.multiple_of((h * 2 + t) * piece + k * tile, tile), tile)
+            value = jnp.dot(act[...], wd[:, columns], preferred_element_type=jnp.float32)
+            store(pl.ds(pl.multiple_of(k * tile, tile), tile), value)
+            return carry
+
+        lax.fori_loop(0, 2, one, 0)
 
     def send_across(dx):
-        a_out[dx] = down(lax.rem(me_h + dx, n_half), other).astype(jnp.bfloat16)
+        def store(columns, value):
+            a_out[dx, :, columns] = value.astype(jnp.bfloat16)
+
+        down(lax.rem(me_h + dx, n_half), other, store)
         a_copies[dx] = go(remote(a_out.at[dx], a_in.at[dx], a_s.at[dx], a_r.at[dx], tp=other))
 
     def send_over(dx):
@@ -553,7 +563,11 @@
     order = [*range(1, n_half), 0]
     for dx in order:
         send_across(dx)
-        mine[dx] = down(lax.rem(me_h + dx, n_half), me_t)
+
+        def keep(columns, value):
+            mine[dx, :, columns] = value
+
+        down(lax.rem(me_h + dx, n_half), me_t, keep)
         send_over(dx)
     for p in reversed(range(n_ep)):
         part = slice(p * block, (p + 1) * block)
@@ -636,7 +650,7 @@
         and n_ep & (n_ep - 1) == 0
         and key_heads == 1
         and hidden_units % LANES == 0
-        and piece % LANES == 0
+        and piece % (2 * LANES) == 0
         and n_half > 1
         and rows % (2 * LANES) == 0
         and requests % (2 * ROW_TILE) == 0

time: 50.3 us -> 51.4 us (1.022)
  Pallas kernels: 48.6 us -> 49.8 us
    pallas_call x1, Pallas kernels: 48.6 us -> 49.8 us  [on_device(): pl.pallas_call(functools.partial(layer_kernel, dict(ep=n_ep, half=n_half)...]
where the time goes in v6:
time: 51.4 us; the launch traced here: 51.3 us
  Pallas kernels  49.8 us (97%)
  local copies, waits for them, and re-layouts  1.47 us (3%)
    pallas_call x1, Pallas kernels, on_device(): pl.pallas_call(functools.partial(layer_kernel, dict(ep=n_ep, half=n_half)...  49.8 us
    unnamed x1, local copies, waits for them, and re-layouts  1.47 us

profile of v6, /device:TPU:0, one launch (start us, length us, event | category | flops | bytes accessed | tf_op | source)
XLA Modules:
  0.0 51.3 jit_solution(3703142275520280094)
XLA Ops:
  0.0 49.8 %shard_map.136 = bf16[64,512]{1,0:T(8,128)(2,1)} custom-call(bf16[32,1024]{1,0:T(8,128)(2,1)} %q_ref.1, bf16[32,128]{1,0:T(8,128)(2,1)} %nk_ref.1, bf16[32,128]{1,0:T(8,128)(2,1)} %nv_ref.1, s32[1,32]{1,0:T(1,128)} %bitcast.13, bf16[64,1024]{1,0:T(8,128)(2,1)} %res_ref.1, f32[1,1024]{1,0:T(1,128)} %bitcast.10, s32[8,64]{1,0:T(8,128)} %bitcast.11, ...), custom_call_target="tpu_custom_call" | custom-call | tf_op jit(solution)/shard_map/pallas_call | solution.py:688
  49.8 1.5 %copy.16 = bf16[64,512]{1,0:T(8,128)(2,1)} copy(bf16[64,512]{1,0:T(8,128)(2,1)} %shard_map.136) | data formatting | bytes 131072
